TPU v7x, 32 devices: a whole 2x2x4 slice. The times are simulated.
32 devices in a mesh: section: 2 (over core), dp: 4 (over z), group: 4 (over y, x).
Axes of the slice: x: 2, y: 2, z: 4, core: 2. Of those that a mesh axis runs over, the one named last changes fastest.
Arguments:
- tokens: bfloat16 [8192, 1024], P(('dp', 'group')), may hold values from -6 to 6
- cotangent: bfloat16 [8192, 1024], P(('dp', 'group')), may hold values from -6 to 6
- mem_keys: bfloat16 [32, 256, 1024], P(('dp', 'group')), may hold values from -6 to 6
- mem_values: bfloat16 [32, 256, 1024], P(('dp', 'group')), may hold values from -6 to 6
- mem_index: int32 [32, 128], P(('dp', 'group')), may hold values from 0 to 255, all different within a row
- mem_flags: int32 [32], P(('dp', 'group')), may hold values 0 or 1
- norm_attn: bfloat16 [2, 1024], P('section'), may hold values from 0.5 to 1.5
- w_qkv: bfloat16 [2, 1024, 3072], P('section'), may hold values from -0.1875 to 0.1875
- w_out: bfloat16 [2, 1024, 1024], P('section'), may hold values from -0.75 to 0.75
- norm_ffn: bfloat16 [2, 1024], P('section'), may hold values from 0.5 to 1.5
- w_gate_up: bfloat16 [2, 1024, 5632], P('section'), may hold values from -0.1875 to 0.1875
- w_down: bfloat16 [2, 2816, 1024], P('section'), may hold values from -0.109375 to 0.109375
Outputs:
- activations: bfloat16 [2, 8192, 1024], P('section', ('dp', 'group'))
- input_grads: bfloat16 [2, 8192, 1024], P('section', ('dp', 'group'))
- grad_norm_attn: float32 [2, 1024], P('section', 'dp')
- grad_w_qkv: float32 [2, 1024, 3072], P('section', 'dp')
- grad_w_out: float32 [2, 1024, 1024], P('section', 'dp')
- grad_norm_ffn: float32 [2, 1024], P('section', 'dp')
- grad_w_gate_up: float32 [2, 1024, 5632], P('section', 'dp')
- grad_w_down: float32 [2, 2816, 1024], P('section', 'dp')
Inputs may be any that keep to these rules, and one draw needn't show every extreme that they name: `mem_index`: each row names 128 different memory rows.
All inputs are finite; a program needn't handle non-finite values. No bound on the sum of `mem_flags` on one device may be relied on, other than what follows from the above.
Results may differ from a plain program's by a relative error of at most 0.03.
Values may be sent and summed in bfloat16 or wider, within the bound.
A program may use at most 256 MiB of HBM per device.

v0:
```python
import jax
import jax.numpy as jnp
from jax import lax
from jax.sharding import PartitionSpec as P

D = 1024
HEADS = 8
HEAD_DIM = 128
FF = 2816
SEG = 256
TOPM = 128
MICRO = 2


EPS = 1e-05
NEG = -1e30


def from_behind(block, axis, distance):
    devices = range(lax.axis_size(axis))
    route = [(i - distance, i) for i in devices if i - distance in devices]
    return lax.ppermute(block, axis, route)


def as_sent(value):

    def short(part):
        return part.astype(jnp.bfloat16) if part.dtype == jnp.float32 else part

    return jax.tree.map(short, value)


def rotary_tables(length, size):
    half = size // 2
    freqs = jnp.exp(-jnp.log(10000.0) * jnp.arange(half, dtype=jnp.float32) * 2.0 / size)
    angles = jnp.arange(length, dtype=jnp.float32)[:, None] * freqs[None, :]
    cosine = jnp.concatenate([jnp.cos(angles), jnp.cos(angles)], axis=1)
    sine = jnp.concatenate([jnp.sin(angles), jnp.sin(angles)], axis=1)
    return (cosine, sine)


def rotate(values, cosine, sine):
    half = values.shape[-1] // 2
    turned = jnp.concatenate([-values[..., half:], values[..., :half]], axis=-1)
    return values * cosine[:, None, :] + turned * sine[:, None, :]


def rotate_back(grads, cosine, sine):
    half = grads.shape[-1] // 2
    moved = grads * sine[:, None, :]
    return grads * cosine[:, None, :] + jnp.concatenate(
        [moved[..., half:], -moved[..., :half]], axis=-1
    )


def contract_rows(left, right):
    return lax.dot_general(
        left, right, (((0,), (0,)), ((), ())), preferred_element_type=jnp.float32
    )


def contract_cols(left, right):
    return lax.dot_general(
        left, right, (((1,), (1,)), ((), ())), preferred_element_type=jnp.float32
    )


def score_blocks(query, key_rot, keys_mem, flags):
    scale = HEAD_DIM ** (-0.5)
    causal = jnp.arange(SEG)[:, None] >= jnp.arange(SEG)[None, :]
    local = (
        jnp.einsum("gqhe,gkhe->ghqk", query, key_rot, preferred_element_type=jnp.float32) * scale
    )
    local = jnp.where(causal, local, NEG)
    remote = (
        jnp.einsum("gqhe,gmhe->ghqm", query, keys_mem, preferred_element_type=jnp.float32) * scale
    )
    remote = jnp.where(flags[:, None, None, None] > 0, remote, NEG)
    return (local, remote)


def forward_layer(layer_input, params, memory):
    gain_attn, weight_qkv, weight_out, gain_ffn, weight_gu, weight_down = params
    keys_mem, values_mem, flags = memory
    row_count = layer_input.shape[0]
    segments = row_count // SEG
    inputs_f = layer_input.astype(jnp.float32)
    first_scale = lax.rsqrt(jnp.mean(inputs_f * inputs_f, axis=-1, keepdims=True) + EPS)
    normed_attn = (inputs_f * first_scale * gain_attn.astype(jnp.float32)).astype(jnp.bfloat16)
    mixed = jnp.dot(normed_attn, weight_qkv, preferred_element_type=jnp.float32)
    mixed = mixed.reshape(segments, SEG, 3, HEADS, HEAD_DIM)
    cosine, sine = rotary_tables(SEG, HEAD_DIM)
    query = rotate(mixed[:, :, 0], cosine, sine).astype(jnp.bfloat16)
    key_rot = rotate(mixed[:, :, 1], cosine, sine).astype(jnp.bfloat16)
    values_loc = mixed[:, :, 2].astype(jnp.bfloat16)
    local, remote = score_blocks(query, key_rot, keys_mem, flags)
    peak_score = jnp.maximum(jnp.max(local, axis=-1), jnp.max(remote, axis=-1))
    totals = jnp.sum(jnp.exp(local - peak_score[..., None]), axis=-1) + jnp.sum(
        jnp.exp(remote - peak_score[..., None]), axis=-1
    )
    log_total = peak_score + jnp.log(totals)
    prob_local = jnp.exp(local - log_total[..., None]).astype(jnp.bfloat16)
    prob_remote = jnp.exp(remote - log_total[..., None]).astype(jnp.bfloat16)
    attended = jnp.einsum(
        "ghqk,gkhe->gqhe", prob_local, values_loc, preferred_element_type=jnp.float32
    )
    attended = attended + jnp.einsum(
        "ghqm,gmhe->gqhe", prob_remote, values_mem, preferred_element_type=jnp.float32
    )
    attended = attended.reshape(row_count, D).astype(jnp.bfloat16)
    resid = inputs_f + jnp.dot(attended, weight_out, preferred_element_type=jnp.float32)
    second_scale = lax.rsqrt(jnp.mean(resid * resid, axis=-1, keepdims=True) + EPS)
    normed_ffn = (resid * second_scale * gain_ffn.astype(jnp.float32)).astype(jnp.bfloat16)
    gate_up = jnp.dot(normed_ffn, weight_gu, preferred_element_type=jnp.float32)
    hidden = (jax.nn.silu(gate_up[:, :FF]) * gate_up[:, FF:]).astype(jnp.bfloat16)
    output = resid + jnp.dot(hidden, weight_down, preferred_element_type=jnp.float32)
    kept = (
        first_scale,
        normed_attn,
        query,
        key_rot,
        values_loc,
        log_total,
        attended,
        resid,
        second_scale,
        normed_ffn,
        gate_up,
        hidden,
    )
    return (output, kept)


def backward_inputs(layer_input, grad_out, kept, params, memory):
    gain_attn, weight_qkv, weight_out, gain_ffn, weight_gu, weight_down = params
    keys_mem, values_mem, flags = memory
    (
        first_scale,
        normed_attn,
        query,
        key_rot,
        values_loc,
        log_total,
        attended,
        resid,
        second_scale,
        normed_ffn,
        gate_up,
        hidden,
    ) = kept
    row_count = layer_input.shape[0]
    segments = row_count // SEG
    inputs_f = layer_input.astype(jnp.float32)
    grad_branch = grad_out.astype(jnp.bfloat16)
    grad_hidden = contract_cols(grad_branch, weight_down)
    gate_part = gate_up[:, :FF]
    up_part = gate_up[:, FF:]
    sigmoid_gate = jax.nn.sigmoid(gate_part)
    grad_gate = grad_hidden * up_part * sigmoid_gate * (1.0 + gate_part * (1.0 - sigmoid_gate))
    grad_up = grad_hidden * gate_part * sigmoid_gate
    grad_gu = jnp.concatenate([grad_gate, grad_up], axis=1).astype(jnp.bfloat16)
    grad_normed = contract_cols(grad_gu, weight_gu)
    scaled_ffn = grad_normed * gain_ffn.astype(jnp.float32)
    grad_gain_ffn = jnp.sum(grad_normed * resid * second_scale, axis=0)
    grad_resid = (
        grad_out
        + second_scale * scaled_ffn
        - resid * second_scale**3 * jnp.mean(scaled_ffn * resid, axis=-1, keepdims=True)
    )
    grad_attn_out = grad_resid.astype(jnp.bfloat16)
    grad_attended = (
        contract_cols(grad_attn_out, weight_out)
        .astype(jnp.bfloat16)
        .reshape(segments, SEG, HEADS, HEAD_DIM)
    )
    local, remote = score_blocks(query, key_rot, keys_mem, flags)
    prob_local = jnp.exp(local - log_total[..., None])
    prob_remote = jnp.exp(remote - log_total[..., None])
    grad_values = jnp.einsum(
        "ghqk,gqhe->gkhe",
        prob_local.astype(jnp.bfloat16),
        grad_attended,
        preferred_element_type=jnp.float32,
    )
    grad_plocal = jnp.einsum(
        "gqhe,gkhe->ghqk", grad_attended, values_loc, preferred_element_type=jnp.float32
    )
    grad_premote = jnp.einsum(
        "gqhe,gmhe->ghqm", grad_attended, values_mem, preferred_element_type=jnp.float32
    )
    centre = jnp.sum(prob_local * grad_plocal, axis=-1) + jnp.sum(
        prob_remote * grad_premote, axis=-1
    )
    grad_slocal = (prob_local * (grad_plocal - centre[..., None])).astype(jnp.bfloat16)
    grad_sremote = (prob_remote * (grad_premote - centre[..., None])).astype(jnp.bfloat16)
    scale = HEAD_DIM ** (-0.5)
    grad_query = scale * (
        jnp.einsum("ghqk,gkhe->gqhe", grad_slocal, key_rot, preferred_element_type=jnp.float32)
        + jnp.einsum("ghqm,gmhe->gqhe", grad_sremote, keys_mem, preferred_element_type=jnp.float32)
    )
    grad_key = scale * jnp.einsum(
        "ghqk,gqhe->gkhe", grad_slocal, query, preferred_element_type=jnp.float32
    )
    cosine, sine = rotary_tables(SEG, HEAD_DIM)
    grad_mixed = jnp.stack(
        [rotate_back(grad_query, cosine, sine), rotate_back(grad_key, cosine, sine), grad_values],
        axis=2,
    )
    grad_mixed = grad_mixed.reshape(row_count, 3 * D).astype(jnp.bfloat16)
    grad_normed_attn = contract_cols(grad_mixed, weight_qkv)
    scaled_attn = grad_normed_attn * gain_attn.astype(jnp.float32)
    grad_gain_attn = jnp.sum(grad_normed_attn * inputs_f * first_scale, axis=0)
    grad_input = (
        grad_resid
        + first_scale * scaled_attn
        - inputs_f * first_scale**3 * jnp.mean(scaled_attn * inputs_f, axis=-1, keepdims=True)
    )
    pending = (
        grad_gain_attn,
        grad_gain_ffn,
        hidden,
        grad_branch,
        normed_ffn,
        grad_gu,
        attended,
        grad_attn_out,
        normed_attn,
        grad_mixed,
    )
    return (grad_input, pending)


def weight_terms(pending):
    (
        grad_gain_attn,
        grad_gain_ffn,
        hidden,
        grad_branch,
        normed_ffn,
        grad_gu,
        attended,
        grad_attn_out,
        normed_attn,
        grad_mixed,
    ) = pending
    return (
        grad_gain_attn,
        contract_rows(normed_attn, grad_mixed),
        contract_rows(attended, grad_attn_out),
        grad_gain_ffn,
        contract_rows(normed_ffn, grad_gu),
        contract_rows(hidden, grad_branch),
    )


def body(
    tokens,
    cotangent,
    mem_keys,
    mem_values,
    mem_index,
    mem_flags,
    norm_attn,
    w_qkv,
    w_out,
    norm_ffn,
    w_gate_up,
    w_down,
):
    params = (norm_attn[0], w_qkv[0], w_out[0], norm_ffn[0], w_gate_up[0], w_down[0])
    upper_section = lax.axis_index("section") == 1
    mb_rows = tokens.shape[0] // MICRO
    mb_segs = mem_flags.shape[0] // MICRO
    picked_keys = jax.vmap(lambda table_rows, picked: jnp.take(table_rows, picked, axis=0))(
        mem_keys, mem_index
    )
    picked_values = jax.vmap(lambda table_rows, picked: jnp.take(table_rows, picked, axis=0))(
        mem_values, mem_index
    )
    picked_keys = picked_keys.reshape(-1, TOPM, HEADS, HEAD_DIM)
    picked_values = picked_values.reshape(-1, TOPM, HEADS, HEAD_DIM)
    live_flags = mem_flags * upper_section.astype(jnp.int32)

    def memory_for(micro):
        start = micro * mb_segs
        return (
            picked_keys[start : start + mb_segs],
            picked_values[start : start + mb_segs],
            live_flags[start : start + mb_segs],
        )

    def rows_of(array, micro):
        return array[micro * mb_rows : (micro + 1) * mb_rows]

    def pick(upper_tree, lower_tree):
        return jax.tree.map(
            lambda upper_leaf, lower_leaf: jnp.where(upper_section, upper_leaf, lower_leaf),
            upper_tree,
            lower_tree,
        )

    def forward_active(operands):
        return forward_layer(operands[0], params, operands[1])

    def forward_spare(operands):
        return jax.tree.map(jnp.zeros_like, forward_active(operands))

    received = jnp.zeros((mb_rows, D), jnp.bfloat16)
    tick_outputs = []
    tick_kept = []
    tick_inputs = []
    for tick_index in range(MICRO + 1):
        lower_micro = min(tick_index, MICRO - 1)
        upper_micro = max(tick_index - 1, 0)
        layer_input = jnp.where(upper_section, received, rows_of(tokens, lower_micro))
        memory = pick(memory_for(upper_micro), memory_for(lower_micro))
        busy = jnp.where(
            upper_section, jnp.asarray(tick_index >= 1), jnp.asarray(tick_index < MICRO)
        )
        output, kept = lax.cond(busy, forward_active, forward_spare, (layer_input, memory))
        output_low = output.astype(jnp.bfloat16)
        if tick_index < MICRO:
            received = from_behind(output_low, "section", 1)
        tick_outputs.append(output_low)
        tick_kept.append(kept)
        tick_inputs.append(layer_input)
    micro_outputs = [pick(tick_outputs[micro + 1], tick_outputs[micro]) for micro in range(MICRO)]

    def backward_active(operands):
        layer_input, grad_out, kept, memory = operands
        grad_input, pending = backward_inputs(layer_input, grad_out, kept, params, memory)
        return (grad_input, pending)

    def backward_spare(operands):
        return jax.tree.map(jnp.zeros_like, backward_active(operands))

    sent_back = jnp.zeros((mb_rows, D), jnp.bfloat16)
    tick_grads = []
    tick_results = []
    for tick_index in range(MICRO + 1):
        upper_micro = min(tick_index, MICRO - 1)
        lower_micro = max(tick_index - 1, 0)
        grad_out = jnp.where(
            upper_section,
            rows_of(cotangent, upper_micro).astype(jnp.float32),
            sent_back.astype(jnp.float32),
        )
        layer_input = pick(tick_inputs[upper_micro + 1], tick_inputs[lower_micro])
        memory = pick(memory_for(upper_micro), memory_for(lower_micro))
        kept = pick(tick_kept[upper_micro + 1], tick_kept[lower_micro])
        busy = jnp.where(
            upper_section, jnp.asarray(tick_index < MICRO), jnp.asarray(tick_index >= 1)
        )
        grad_input, result = lax.cond(
            busy, backward_active, backward_spare, (layer_input, grad_out, kept, memory)
        )
        grad_low = grad_input.astype(jnp.bfloat16)
        if tick_index < MICRO:
            sent_back = from_behind(grad_low, "section", -1)
        tick_grads.append(grad_low)
        tick_results.append(result)
    micro_results = [pick(tick_results[micro], tick_results[micro + 1]) for micro in range(MICRO)]
    gain_attn_sum = micro_results[0][0]
    gain_ffn_sum = micro_results[0][1]
    micro = 1
    gain_attn_sum = gain_attn_sum + micro_results[micro][0]
    gain_ffn_sum = gain_ffn_sum + micro_results[micro][1]
    joined = tuple(
        (jnp.concatenate([item[slot] for item in micro_results], axis=0) for slot in range(2, 10))
    )
    grad_sums = weight_terms((gain_attn_sum, gain_ffn_sum) + joined)
    micro_grads = [pick(tick_grads[micro], tick_grads[micro + 1]) for micro in range(MICRO)]
    activations = jnp.concatenate(micro_outputs, axis=0)[None]
    input_grads = jnp.concatenate(micro_grads, axis=0)[None]
    stacked = tuple((item[None] for item in grad_sums))
    shards = jax.tree.map(
        lambda part: part.astype(jnp.float32),
        lax.psum_scatter(as_sent(stacked), "dp", scatter_dimension=1, tiled=True),
    )
    totals = jax.tree.map(lambda part: part.astype(jnp.float32), lax.psum(as_sent(shards), "group"))
    return (
        activations,
        input_grads,
        totals[0],
        totals[1],
        totals[2],
        totals[3],
        totals[4],
        totals[5],
    )


def solution(mesh):
    placed = (
        P(("dp", "group"), None),
        P(("dp", "group"), None),
        P(("dp", "group"), None, None),
        P(("dp", "group"), None, None),
        P(("dp", "group"), None),
        P(("dp", "group")),
        P("section", None),
        P("section", None, None),
        P("section", None, None),
        P("section", None),
        P("section", None, None),
        P("section", None, None),
    )
    return jax.shard_map(
        body,
        mesh=mesh,
        in_specs=placed,
        out_specs=(
            P("section", ("dp", "group"), None),
            P("section", ("dp", "group"), None),
            P("section", "dp"),
            P("section", "dp", None),
            P("section", "dp", None),
            P("section", "dp"),
            P("section", "dp", None),
            P("section", "dp", None),
        ),
        check_vma=False,
    )
```

profile of v0, /device:TPU:0, one launch (start us, length us, event | category | flops | bytes accessed | tf_op | source)
XLA Modules:
  0.0 1044.6 jit_solution(11970865667284336876)
XLA Ops:
  12.5 3.6 gather_fusion.1
  17.4 2.8 gather_fusion
  25.1 51.1 %conditional.4 = (f32[256,1]{0,1:T(1,128)S(1)}, bf16[256,1024]{1,0:T(8,128)(2,1)}, bf16[1,256,8,128]{3,1,2,0:T(8,128)(2,1)}, bf16[1,256,8,128]{3,1,2,0:T(8,128)(...) conditional(s32[]{:T(128)} %convert_element_type.543, () %tuple.69, ...), branch_computations={%region_0.0_spmd, %region_1.9_spmd} | conditional | flops 6999523840 | bytes 128566280 | solution.py:320
  29.7 4.8 convolution_bitcast_fusion
  51.6 2.8 multiply_reduce_fusion
  54.4 2.3 multiply_convert_fusion
  56.7 10.2 fusion.264
  67.0 4.6 fusion
  71.6 4.2 fusion.3
  81.8 8.7 copy.301
  100.4 4.9 convolution_bitcast_fusion.8
  109.1 2.9 convert_add_fusion.2
  113.5 9.5 fusion.234
  123.0 4.6 fusion.148
  127.7 4.0 fusion.161
  138.7 18.3 %conditional.6 = (f32[1024]{0:T(1024)S(1)}, f32[1024]{0:T(1024)S(1)}, bf16[256,2816]{1,0:T(8,128)(2,1)S(1)}, bf16[256,1024]{1,0:T(8,128)(2,1)S(1)}, bf16[256,102...) conditional(s32[]{:T(128)} %convert_element_type.544, () %tuple.73, ...), branch_computations={%region_22.24_spmd, %region_23.31_spmd} | conditional | flops 7488881664 | bytes 230749824 | solution.py:354
  160.3 20.8 %conditional.5 = (f32[256,1]{0,1:T(1,128)S(1)}, bf16[256,1024]{1,0:T(8,128)(2,1)S(1)}, bf16[1,256,8,128]{3,1,2,0:T(8,128)(2,1)S(1)}, bf16[1,256,8,128]{3,1,2,0:T...) conditional(s32[]{:T(128)} %convert_element_type.544, () %tuple.71, ...), branch_computations={%region_14.16_spmd, %region_15.23_spmd} | conditional | flops 6999523840 | bytes 140104896 | solution.py:320
  168.0 3.2 broadcast.746
  184.8 3.5 broadcast_select_fusion.13
  188.4 3.0 collective-permute-done.2
  191.4 4.0 fusion.147
  195.5 10.4 multiply_reduce_fusion.11
  205.9 3.2 broadcast_select_fusion.29
  223.1 5.6 fusion.173
  231.3 67.9 %collective-permute-done.3 = bf16[256,1024]{1,0:T(8,128)(2,1)S(1)} collective-permute-done((bf16[256,1024]{1,0:T(8,128)(2,1)S(1)}, bf16[256,1024]{1,0:T(8,128)(2,1)S(1)}, u32[]{:S(2)}, u32[]{:S(2)}) %collective-permute-start.3) | collective-permute-done | bytes 524320 | tf_op jit(solution)/shard_map/ppermute | solution.py:22
  300.3 67.7 %conditional.7 = (f32[1024]{0:T(1024)S(1)}, f32[1024]{0:T(1024)S(1)}, bf16[256,2816]{1,0:T(8,128)(2,1)S(1)}, bf16[256,1024]{1,0:T(8,128)(2,1)S(1)}, bf16[256,102...) conditional(s32[]{:T(128)} %convert_element_type.543, () %tuple.75, ...), branch_computations={%region_34.36_spmd, %region_35.43_spmd} | conditional | flops 7488881664 | bytes 220264160 | solution.py:354
  318.1 2.5 broadcast_select_fusion.7
  320.7 3.7 select_n.468
  324.4 5.4 select_n.462
  329.7 5.4 fusion.102
  336.4 9.3 multiply_reduce_fusion.7
  361.2 5.0 fusion.114
  369.0 2.7 broadcast_select_fusion.26
  371.8 2.7 convert_bitcast_fusion.5
  378.2 5.0 convert_bitcast_fusion.4
  387.6 5.6 convert_bitcast_fusion.3
  394.6 3.0 broadcast_select_fusion.12
  397.5 9.1 convert_bitcast_fusion.2
  409.3 11.8 %reduce-scatter.13.cloned.1.call-done = bf16[1,256,1024]{2,1,0:T(8,128)(2,1)} async-done(((bf16[1,1024,1024]{2,1,0:T(8,128)(2,1)}), bf16[1,256,1024]{2,1,0:T(8,128)(2,1)}) %reduce-scatter.13.cloned.1.call-update) | async-done | bytes 524304 | tf_op jit(solution)/shard_map/reduce_scatter | solution.py:378
  421.1 104.7 %reduce-scatter.17.cloned.1.call-done = bf16[1,704,1024]{2,1,0:T(8,128)(2,1)} async-done(((bf16[1,2816,1024]{2,1,0:T(8,128)(2,1)}), bf16[1,704,1024]{2,1,0:T(8,128)(2,1)}) %reduce-scatter.17.cloned.1.call-update) | async-done | bytes 1441808 | tf_op jit(solution)/shard_map/reduce_scatter | solution.py:378
  525.8 113.7 %reduce-scatter.11.cloned.1.call-done = bf16[1,256,3072]{2,1,0:T(8,128)(2,1)} async-done(((bf16[1,1024,3072]{2,1,0:T(8,128)(2,1)}), bf16[1,256,3072]{2,1,0:T(8,128)(2,1)}) %reduce-scatter.11.cloned.1.call-update) | async-done | bytes 1572880 | tf_op jit(solution)/shard_map/reduce_scatter | solution.py:378
  639.5 197.8 %reduce-scatter.15.cloned.1.call-done = bf16[1,256,5632]{2,1,0:T(8,128)(2,1)} async-done(((bf16[1,1024,5632]{2,1,0:T(8,128)(2,1)}), bf16[1,256,5632]{2,1,0:T(8,128)(2,1)}) %reduce-scatter.15.cloned.1.call-update) | async-done | bytes 2883600 | tf_op jit(solution)/shard_map/reduce_scatter | solution.py:378
  841.9 18.9 %reduce-scatter.19.cloned.1.call-done = bf16[256,1]{1,0:T(8,128)(2,1)} async-done(((bf16[1024,1]{1,0:T(8,128)(2,1)}), bf16[256,1]{1,0:T(8,128)(2,1)}) %reduce-scatter.19.cloned.1.call-update) | async-done | bytes 528
  861.7 19.7 %reduce-scatter.21.cloned.1.call-done = bf16[256,1]{1,0:T(8,128)(2,1)} async-done(((bf16[1024,1]{1,0:T(8,128)(2,1)}), bf16[256,1]{1,0:T(8,128)(2,1)}) %reduce-scatter.21.cloned.1.call-update) | async-done | bytes 528
  882.4 10.0 all-reduce
  893.5 132.3 %all-reduce.4.cloned.1.call-done = (bf16[1,256,3072]{2,1,0:T(8,128)(2,1)}, bf16[1,256,1024]{2,1,0:T(8,128)(2,1)}, bf16[1,256,5632]{2,1,0:T(8,128)(2,1)}, bf16[1,704,1024]{2,1,0:T(8,128)(2,1)}) async-done(((bf16[1,256,3072]{2,1,0:T(8,128)(2,1)}, bf16[1,256,1024]{2,1,0:T(8,128)(2,1)}, bf16[1,256,5632]{2,1,0:T(8,128)(2,1)}, bf16[1,704,1024]{2,1,0:T(8,128)(2,1)}), (bf16[1,256,3072]{2,1,0:T(8,128)(2,1)}, ...) | async-done | bytes 6422544 | tf_op jit(solution)/shard_map/psum | solution.py:380
  1028.0 3.4 convert_element_type.584
  1034.3 3.2 convert_element_type.593
  (489 shorter events, 157.3 us)
Async XLA Ops:
  7.2 414.0 %reduce-scatter.13.cloned.1.call-start = ((), (), s32[]{:S(2)}) async-start(), calls=%async_computation.7 | async-start | bytes 2621440 | tf_op jit(solution)/shard_map/reduce_scatter | solution.py:378
  10.7 71.1 %copy-start.122 = (bf16[1024]{0:T(1024)(128)(2,1)}, bf16[1024]{0:T(1024)(128)(2,1)S(1)}, u32[]{:S(2)}) copy-start(bf16[1024]{0:T(1024)(128)(2,1)S(1)} %reduce.46) | copy-start | bytes 6148
  11.4 69.8 %copy-start.125 = (bf16[1024]{0:T(1024)(128)(2,1)}, bf16[1024]{0:T(1024)(128)(2,1)S(1)}, u32[]{:S(2)}) copy-start(bf16[1024]{0:T(1024)(128)(2,1)S(1)} %reduce.47) | copy-start | bytes 6148
  12.5 11.9 %copy-start.16 = (bf16[256,1024]{1,0:T(8,128)(2,1)}, bf16[256,1024]{1,0:T(8,128)(2,1)S(1)}, u32[]{:S(2)}) copy-start(bf16[256,1024]{1,0:T(8,128)(2,1)S(1)} %slice_select_fusion) | copy-start | bytes 1572868
  25.3 9.1 copy-start.17
  26.1 8.3 copy-start.158
  54.4 12.6 %copy-start.167 = (f32[256]{0:T(256)}, f32[256]{0:T(256)S(1)}, u32[]{:S(2)}) copy-start(f32[256]{0:T(256)S(1)} %add_rsqrt_fusion) | copy-start | bytes 3076 | tf_op jit(solution)/shard_map/cond
  54.4 17.2 %slice-start.2 = ((s8[5767168]{0:T(1024)(128)(4,1)}), s8[4194304]{0:T(1024)(128)(4,1)S(1)}, s32[]{:S(2)}) async-start(s8[5767168]{0:T(1024)(128)(4,1)} %bitcast.562), calls=%async_computation.15 | async-start | bytes 8388608 | tf_op jit(solution)/shard_map/cond
  56.7 14.9 %slice-start.3 = ((s8[5767168]{0:T(1024)(128)(4,1)}), s8[1572864]{0:T(1024)(128)(4,1)S(1)}, s32[]{:S(2)}) async-start(s8[5767168]{0:T(1024)(128)(4,1)} %bitcast.562), calls=%async_computation.16 | async-start | bytes 3145728 | tf_op jit(solution)/shard_map/cond
  76.2 21.9 %collective-permute-start = (bf16[256,1024]{1,0:T(8,128)(2,1)}, bf16[256,1024]{1,0:T(8,128)(2,1)}, u32[]{:S(2)}, u32[]{:S(2)}) collective-permute-start(bf16[256,1024]{1,0:T(8,128)(2,1)} %get-tuple-element.674), channel_id=1, source_target_pairs={{0,16},{1,17},{2,18},{3,19},{4,20},{5,21},{6,22},{7,23},{8,24},{9,... | collective-permute-start | bytes 1572872 | tf_op jit(solution)/shard_map/ppermute | solution.py:22
  78.7 28.3 %copy-start.100 = (pred[256,256]{0,1:T(8,128)(4,1)}, pred[256,256]{0,1:T(8,128)(4,1)S(1)}, u32[]{:S(2)}) copy-start(pred[256,256]{0,1:T(8,128)(4,1)S(1)} %iota_compare_fusion.4) | copy-start | bytes 196612
  81.8 17.3 %copy-start.130 = (f32[1024]{0:T(1024)}, f32[1024]{0:T(1024)S(1)}, u32[]{:S(2)}) copy-start(f32[1024]{0:T(1024)S(1)} %convert_element_type.546) | copy-start | bytes 12292
  90.5 7.7 copy-start.60
  99.2 39.4 %copy-start.138 = (f32[256]{0:T(256)}, f32[256]{0:T(256)S(1)}, u32[]{:S(2)}) copy-start(f32[256]{0:T(256)S(1)} %add_rsqrt_fusion.5) | copy-start | bytes 3076
  108.2 30.4 %copy-start.118 = (f32[8,256]{1,0:T(8,128)}, f32[8,256]{1,0:T(8,128)S(1)}, u32[]{:S(2)}) copy-start(f32[8,256]{1,0:T(8,128)S(1)} %log_add_fusion.2) | copy-start | bytes 24580
  112.1 26.5 %copy-start.140 = (f32[256]{0:T(256)}, f32[256]{0:T(256)S(1)}, u32[]{:S(2)}) copy-start(f32[256]{0:T(256)S(1)} %add_rsqrt_fusion.4) | copy-start | bytes 3076
  112.1 15.6 %slice-start = ((s8[5767168]{0:T(1024)(128)(4,1)}), s8[4194304]{0:T(1024)(128)(4,1)S(1)}, s32[]{:S(2)}) async-start(s8[5767168]{0:T(1024)(128)(4,1)} %bitcast.559), calls=%async_computation.13 | async-start | bytes 8388608
  113.5 25.1 %copy-start.23 = (bf16[256,1024]{1,0:T(8,128)(2,1)}, bf16[256,1024]{1,0:T(8,128)(2,1)S(1)}, u32[]{:S(2)}) copy-start(bf16[256,1024]{1,0:T(8,128)(2,1)S(1)} %fusion.164) | copy-start | bytes 1572868
  113.5 14.1 %slice-start.1 = ((s8[5767168]{0:T(1024)(128)(4,1)}), s8[1572864]{0:T(1024)(128)(4,1)S(1)}, s32[]{:S(2)}) async-start(s8[5767168]{0:T(1024)(128)(4,1)} %bitcast.559), calls=%async_computation.14 | async-start | bytes 3145728
  131.7 26.6 %collective-permute-start.1 = (bf16[256,1024]{1,0:T(8,128)(2,1)}, bf16[256,1024]{1,0:T(8,128)(2,1)}, u32[]{:S(2)}, u32[]{:S(2)}) collective-permute-start(bf16[256,1024]{1,0:T(8,128)(2,1)} %fusion.161), channel_id=1, source_target_pairs={{0,16},{1,17},{2,18},{3,19},{4,20},{5,21},{6,22},{7,23},{8,24},{9,... | collective-permute-start | bytes 1572872 | tf_op jit(solution)/shard_map/ppermute | solution.py:22
  157.1 34.3 %collective-permute-start.2 = (bf16[256,1024]{1,0:T(8,128)(2,1)}, bf16[256,1024]{1,0:T(8,128)(2,1)}, u32[]{:S(2)}, u32[]{:S(2)}) collective-permute-start(bf16[256,1024]{1,0:T(8,128)(2,1)} %get-tuple-element.688), channel_id=1, source_target_pairs={{16,0},{17,1},{18,2},{19,3},{20,4},{21,5},{22,6},{23,7},{24,8},{25... | collective-permute-start | bytes 1572872 | tf_op jit(solution)/shard_map/ppermute | solution.py:22
  188.4 7.1 copy-start.129
  195.4 10.4 copy-start.93
  195.4 10.4 copy-start.95
  195.5 10.4 copy-start.84
  195.5 10.4 copy-start.88
  221.8 6.8 copy-start.28
  228.7 71.6 %copy-start.119 = (f32[8,256]{1,0:T(8,128)S(1)}, f32[8,256]{1,0:T(8,128)}, u32[]{:S(2)}) copy-start(f32[8,256]{1,0:T(8,128)} %copy-done.118) | copy-start | bytes 24580
  228.7 71.6 %copy-start.124 = (bf16[1024]{0:T(1024)(128)(2,1)S(1)}, bf16[1024]{0:T(1024)(128)(2,1)}, u32[]{:S(2)}) copy-start(bf16[1024]{0:T(1024)(128)(2,1)} %copy-done.122) | copy-start | bytes 6148
  228.7 71.6 %copy-start.127 = (bf16[1024]{0:T(1024)(128)(2,1)S(1)}, bf16[1024]{0:T(1024)(128)(2,1)}, u32[]{:S(2)}) copy-start(bf16[1024]{0:T(1024)(128)(2,1)} %copy-done.125) | copy-start | bytes 6148
  228.7 71.6 %copy-start.133 = (pred[1,8,256]{2,1,0:T(8,128)(4,1)S(1)}, pred[1,8,256]{2,1,0:T(8,128)(4,1)}, u32[]{:S(2)}) copy-start(pred[1,8,256]{2,1,0:T(8,128)(4,1)} %copy-done.132) | copy-start | bytes 6148
  228.7 71.6 %copy-start.139 = (f32[256]{0:T(256)S(1)}, f32[256]{0:T(256)}, u32[]{:S(2)}) copy-start(f32[256]{0:T(256)} %copy-done.138) | copy-start | bytes 3076
  228.7 71.6 %copy-start.141 = (f32[256]{0:T(256)S(1)}, f32[256]{0:T(256)}, u32[]{:S(2)}) copy-start(f32[256]{0:T(256)} %copy-done.140) | copy-start | bytes 3076
  228.7 71.6 %copy-start.166 = (f32[256,1]{0,1:T(1,128)S(1)}, f32[256,1]{0,1:T(1,128)}, u32[]{:S(2)}) copy-start(f32[256,1]{0,1:T(1,128)} %copy-done.165) | copy-start | bytes 3076
  228.7 71.6 %copy-start.177 = (pred[256,1]{0,1:T(4,128)(4,1)S(1)}, pred[256,1]{0,1:T(4,128)(4,1)}, u32[]{:S(2)}) copy-start(pred[256,1]{0,1:T(4,128)(4,1)} %copy-done.176) | copy-start | bytes 772
  230.0 70.3 %copy-start.81 = (bf16[256,1024]{1,0:T(8,128)(2,1)}, bf16[256,1024]{1,0:T(8,128)(2,1)S(1)}, u32[]{:S(2)}) copy-start(bf16[256,1024]{1,0:T(8,128)(2,1)S(1)} %get-tuple-element.1156) | copy-start | bytes 1572868
  230.0 69.2 %collective-permute-start.3 = (bf16[256,1024]{1,0:T(8,128)(2,1)S(1)}, bf16[256,1024]{1,0:T(8,128)(2,1)S(1)}, u32[]{:S(2)}, u32[]{:S(2)}) collective-permute-start(bf16[256,1024]{1,0:T(8,128)(2,1)S(1)} %get-tuple-element.1156), channel_id=1, source_target_pairs={{16,0},{17,1},{18,2},{19,3},{20,4},{21,5},{22,6},{23,7},{24,8},{25... | collective-permute-start | bytes 1572872 | tf_op jit(solution)/shard_map/ppermute | solution.py:22
  320.6 9.1 copy-start.69
  336.3 9.3 copy-start.11
  336.4 9.3 copy-start.12
  336.4 9.3 copy-start.13
  336.4 9.3 copy-start.180
  374.5 151.3 %reduce-scatter.17.cloned.1.call-start = ((), (), s32[]{:S(2)}) async-start(), calls=%async_computation.9 | async-start | bytes 7208960 | tf_op jit(solution)/shard_map/reduce_scatter | solution.py:378
  383.2 256.3 %reduce-scatter.11.cloned.1.call-start = ((), (), s32[]{:S(2)}) async-start(), calls=%async_computation.6 | async-start | bytes 7864320 | tf_op jit(solution)/shard_map/reduce_scatter | solution.py:378
  393.2 444.1 %reduce-scatter.15.cloned.1.call-start = ((), (), s32[]{:S(2)}) async-start(), calls=%async_computation.8 | async-start | bytes 14417920 | tf_op jit(solution)/shard_map/reduce_scatter | solution.py:378
  406.7 454.1 %reduce-scatter.19.cloned.1.call-start = ((), (), s32[]{:S(2)}) async-start(), calls=%async_computation.10 | async-start | bytes 327680
  408.3 473.2 %reduce-scatter.21.cloned.1.call-start = ((), (), s32[]{:S(2)}) async-start(), calls=%async_computation.11 | async-start | bytes 327680
  409.3 616.5 %all-reduce.4.cloned.1.call-start = ((), (), s32[]{:S(2)}) async-start(), calls=%async_computation.12 | async-start | bytes 12845056 | tf_op jit(solution)/shard_map/psum | solution.py:380
  (107 other events, 264.9 us)
Sparse Core Ops, SparseCore 0:
  374.6 46.4 reduce-scatter.12
  424.1 101.6 reduce-scatter.16
  528.2 111.2 reduce-scatter.10
  641.8 195.4 reduce-scatter.14
  840.1 20.6 reduce-scatter.18
  863.5 17.9 reduce-scatter.20
  885.8 139.9 all-reduce.3
where the time goes:
time: 1050 us; the launch traced here: 1040 us
  waiting for transfers between devices  670 us (64%)
  matrix products  127 us (12%)
  other arithmetic  101 us (10%)
  local copies, waits for them, and re-layouts  88.3 us (8%)
  loops' own time  23.6 us (2%)
  between operations  18.1 us (2%)
    reduce_scatter x4, waiting for transfers between devices, body(): lax.psum_scatter(as_sent(stacked), 'dp', scatter_dimension=1, tiled=True)  428 us
    psum x1, waiting for transfers between devices, body(): lax.psum(as_sent(shards), 'group')  132 us
    ppermute x4, waiting for transfers between devices, from_behind(): return lax.ppermute(block, axis, route)  70.9 us
    dot_general x8, matrix products, contract_cols(): lax.dot_general(left, right, (((1,), (1,)), ((), ())), preferred_element_...  42.7 us
    select_n x20, other arithmetic, pick(): jnp.where(upper_section, upper_leaf, lower_leaf)  39.8 us
    unnamed x9, waiting for transfers between devices  38.8 us
    another operation x32, local copies, waits for them, and re-layouts  27.8 us
    dot_general x4, matrix products, contract_rows(): lax.dot_general(left, right, (((0,), (0,)), ((), ())), preferred_element_...  22.4 us
  transfers between devices with their start and end apart: 11, of which 9 were waited for; matrix products, arithmetic and copies ran while one was open for 8% of the time, Pallas kernels for 0%

commit v1 on v0

--- a/solution.py
+++ b/solution.py
@@ -1,6 +1,10 @@
+import functools
+
 import jax
 import jax.numpy as jnp
 from jax import lax
+from jax.experimental import pallas as pl
+from jax.experimental.pallas import tpu as pltpu
 from jax.sharding import PartitionSpec as P
 
 D = 1024
@@ -14,20 +18,13 @@
 
 EPS = 1e-05
 NEG = -1e30
+MESH = pl.DeviceIdType.MESH
 
 
 def from_behind(block, axis, distance):
     devices = range(lax.axis_size(axis))
     route = [(i - distance, i) for i in devices if i - distance in devices]
     return lax.ppermute(block, axis, route)
-
-
-def as_sent(value):
-
-    def short(part):
-        return part.astype(jnp.bfloat16) if part.dtype == jnp.float32 else part
-
-    return jax.tree.map(short, value)
 
 
 def rotary_tables(length, size):
@@ -50,12 +47,6 @@
     moved = grads * sine[:, None, :]
     return grads * cosine[:, None, :] + jnp.concatenate(
         [moved[..., half:], -moved[..., :half]], axis=-1
-    )
-
-
-def contract_rows(left, right):
-    return lax.dot_general(
-        left, right, (((0,), (0,)), ((), ())), preferred_element_type=jnp.float32
     )
 
 
@@ -230,30 +221,380 @@
     return (grad_input, pending)
 
 
-def weight_terms(pending):
-    (
-        grad_gain_attn,
-        grad_gain_ffn,
-        hidden,
-        grad_branch,
-        normed_ffn,
-        grad_gu,
-        attended,
-        grad_attn_out,
-        normed_attn,
-        grad_mixed,
-    ) = pending
+BLOCK = 256
+LAG = 2
+
+
+def flip(value, mask):
+    return value + mask * (1 - 2 * ((value // mask) % 2))
+
+
+def summed(left, right):
+    return (left.astype(jnp.float32) + right.astype(jnp.float32)).astype(jnp.bfloat16)
+
+
+def reduce_kernel(extra, *refs):
+    n_extra = len(extra)
+    (nf_t, na_t, o_t, z_t, dgu, dm, f_cols, e_cols, gains) = refs[:9]
+    (out_sq, out_d, out_gains) = refs[9:12]
+    refs = refs[12:]
+    (a_own, a_in, z_own, z_in, b_own, b_in, e_own, e_in) = refs[:8]
+    (g_sq, q0, q1, q2, g_d, d0, d1, d2, gain_out, gain_in) = refs[8:18]
+    refs = refs[18:]
+    x_sq, x_d = refs[:2]
+    (sem_load, sem_bload, sem_asend, sem_arecv, sem_bsend, sem_brecv) = refs[2:8]
+    (sem_send, sem_recv, sem_copy, gain_send, gain_recv) = refs[8:13]
+
+    section, dpi, group = (lax.axis_index(name) for name in ("section", "dp", "group"))
+    mask1 = 1 + section
+    mask2 = 2 - section
+    half = (group // mask1) % 2
+    low2 = (group // mask2) % 2
+    bit0 = dpi % 2
+    bit1 = (dpi // 2) % 2
+    first = (section, dpi, flip(group, mask1))
+    second = (section, dpi, flip(group, mask2))
+    near = (section, flip(dpi, 1), group)
+    far = (section, flip(dpi, 2), group)
+    others = [(section, dpi, flip(group, mask)) for mask in extra]
+    partners = [first, second, near, far] + others
+
+    barrier = pltpu.get_barrier_semaphore()
+    for partner in partners:
+        pl.semaphore_signal(barrier, inc=1, device_id=partner, device_id_type=MESH)
+    pl.semaphore_wait(barrier, len(partners))
+
+    def remote(src, dst, send, recv, device):
+        return pltpu.make_async_remote_copy(
+            src_ref=src, dst_ref=dst, send_sem=send, recv_sem=recv, device_id=device, device_id_type=MESH
+        )
+
+    def load_a(slot):
+        src = (nf_t, o_t, na_t)[slot]
+        return pltpu.make_async_copy(src, a_own.at[slot], sem_load.at[slot])
+
+    def load_z():
+        return pltpu.make_async_copy(z_t.at[pl.ds(0, 4), half], z_own, sem_load.at[3])
+
+    def b_src(index, part):
+        if index[0] == 0:
+            return dgu.at[part * 11 + index[1]]
+        if index[0] == 1:
+            return f_cols.at[part * 2 + index[1]]
+        return dm.at[part * 6 + index[1]]
+
+    def load_b(kind, i, slot):
+        return pltpu.make_async_copy(b_src((kind, i), half), b_own.at[slot], sem_bload.at[slot])
+
+    def load_e(k):
+        return pltpu.make_async_copy(e_cols.at[k], e_own.at[k], sem_bload.at[19 + k])
+
+    def send_a(slot):
+        src = (nf_t, o_t, na_t)[slot]
+        return remote(src, a_in.at[slot], sem_asend.at[slot], sem_arecv.at[slot], first)
+
+    def send_z():
+        return remote(z_t.at[pl.ds(0, 4), 1 - half], z_in, sem_asend.at[3], sem_arecv.at[3], first)
+
+    def send_b(kind, i, slot):
+        return remote(b_src((kind, i), 1 - half), b_in.at[slot], sem_bsend.at[slot], sem_brecv.at[slot], first)
+
+    def send_e(k):
+        return remote(e_cols.at[k], e_in.at[k], sem_bsend.at[19 + k], sem_brecv.at[19 + k], first)
+
+    kinds = ((0, 0, 11), (1, 11, 2), (2, 13, 6))
+    load_z().start()
+    send_z().start()
+
+    @pl.loop(0, 4)
+    def _(k):
+        load_e(k).start()
+        send_e(k).start()
+
+    for kind, base, count in kinds:
+        load_a(kind).start()
+        send_a(kind).start()
+
+        @pl.loop(0, count)
+        def _(i):
+            load_b(kind, i, base + i).start()
+            send_b(kind, i, base + i).start()
+
+    class Square:
+        base, rows = 4, 256
+        partial, recv0, recv1, recv2, xs, out = g_sq, q0, q1, q2, x_sq, out_sq
+
+    class Down:
+        base, rows = 0, 352
+        partial, recv0, recv1, recv2, xs, out = g_d, d0, d1, d2, x_d, out_d
+
+    def to_near(cls, c):
+        k = cls.base + c
+        return remote(cls.partial.at[c, pl.ds(0, 2), 1 - bit0], cls.recv0.at[c], sem_send.at[0, k], sem_recv.at[0, k], near)
+
+    def to_far(cls, c):
+        k = cls.base + c
+        return remote(cls.recv0.at[c, 1 - bit1], cls.recv1.at[c], sem_send.at[1, k], sem_recv.at[1, k], far)
+
+    def rows_at(cls, part):
+        size = cls.rows // 2
+        return pl.ds(pl.multiple_of(part * size, 16), size)
+
+    def to_second(cls, c):
+        k = cls.base + c
+        return remote(cls.recv1.at[c, rows_at(cls, 1 - low2)], cls.recv2.at[c], sem_send.at[2, k], sem_recv.at[2, k], second)
+
+    def to_extra(cls, c, i):
+        k = cls.base + c
+        src = cls.recv2.at[c] if i == 0 else cls.xs.at[i - 1, c]
+        return remote(src, cls.xs.at[i, c], sem_send.at[6 + i, k], sem_recv.at[6 + i, k], others[i])
+
+    def final(cls, c):
+        return cls.recv2.at[c] if n_extra == 0 else cls.xs.at[n_extra - 1, c]
+
+    def share_second(cls, c):
+        k = cls.base + c
+        return remote(final(cls, c), cls.out.at[half, c, rows_at(cls, low2)], sem_send.at[3, k], sem_recv.at[3, k], second)
+
+    def share_first(cls, c):
+        k = cls.base + c
+        return remote(final(cls, c), cls.out.at[half, c, rows_at(cls, low2)], sem_send.at[4, k], sem_recv.at[4, k], first)
+
+    def pass_on(cls, c):
+        k = cls.base + c
+        block = cls.out.at[half, c, rows_at(cls, 1 - low2)]
+        return remote(block, block, sem_send.at[5, k], sem_recv.at[5, k], first)
+
+    def keep(cls, c):
+        return pltpu.make_async_copy(final(cls, c), cls.out.at[half, c, rows_at(cls, low2)], sem_copy.at[cls.base + c])
+
+    def multiply(left, right, left2, right2):
+        total = jnp.dot(left, right, preferred_element_type=jnp.float32)
+        total += jnp.dot(left2, right2, preferred_element_type=jnp.float32)
+        return total.astype(jnp.bfloat16)
+
+    def partial_square(c):
+        for kind, base, count in kinds:
+
+            @pl.when(c == base)
+            def _():
+                load_a(kind).wait()
+                send_a(kind).wait_recv()
+
+        load_b(0, 0, c).wait()
+        send_b(0, 0, c).wait_recv()
+        for kind, base, count in kinds:
+
+            @pl.when((c >= base) & (c < base + count))
+            def _():
+                for j in range(4):
+                    rows = pl.ds(j * 256, 256)
+                    g_sq[c, j // 2, j % 2] = multiply(
+                        a_own[kind, rows, :], b_own[c], a_in[kind, rows, :], b_in[c]
+                    )
+
+        to_near(Square, c).start()
+
+    def partial_down(c):
+        @pl.when(c == 0)
+        def _():
+            load_z().wait()
+            send_z().wait_recv()
+
+        load_e(c).wait()
+        send_e(c).wait_recv()
+        for j in range(4):
+            g_d[c, j // 2, j % 2] = multiply(z_own[j], e_own[c], z_in[j], e_in[c])
+        to_near(Down, c).start()
+
+    def stage_near(cls, c):
+        to_near(cls, c).wait_recv()
+        for i in range(2):
+            cls.recv0[c, i] = summed(cls.partial[c, i, bit0], cls.recv0[c, i])
+        to_far(cls, c).start()
+
+    def stage_far(cls, c):
+        to_far(cls, c).wait_recv()
+        cls.recv1[c] = summed(cls.recv0[c, bit1], cls.recv1[c])
+        to_second(cls, c).start()
+
+    def share(cls, c):
+        share_second(cls, c).start()
+        share_first(cls, c).start()
+        keep(cls, c).start()
+
+    def stage_second(cls, c):
+        to_second(cls, c).wait_recv()
+        cls.recv2[c] = summed(cls.recv1[c, rows_at(cls, low2)], cls.recv2[c])
+        if n_extra:
+            to_extra(cls, c, 0).start()
+        else:
+            share(cls, c)
+
+    def stage_extra(cls, c, i):
+        to_extra(cls, c, i).wait()
+        mine = cls.recv2[c] if i == 0 else cls.xs[i - 1, c]
+        cls.xs[i, c] = summed(mine, cls.xs[i, c])
+        if i + 1 < n_extra:
+            to_extra(cls, c, i + 1).start()
+        else:
+            share(cls, c)
+
+    def stage_pass(cls, c):
+        share_second(cls, c).wait_recv()
+        pass_on(cls, c).start()
+
+    def partial(cls, c):
+        (partial_square if cls is Square else partial_down)(c)
+
+    stages = [partial, stage_near, stage_far, stage_second]
+    stages += [functools.partial(lambda i, cls, c: stage_extra(cls, c, i), i) for i in range(n_extra)]
+    stages += [stage_pass]
+
+    def gain_exchange(i):
+        return remote(gain_out.at[i], gain_in.at[i], gain_send.at[i], gain_recv.at[i], partners[i])
+
+    steps = 23 + LAG * (len(stages) - 1)
+
+    @pl.loop(0, steps)
+    def _(t):
+        for i, stage in enumerate(stages):
+            c = t - LAG * i
+
+            @pl.when((c >= 0) & (c < 4))
+            def _():
+                stage(Down, c)
+
+            @pl.when((c >= 4) & (c < 23))
+            def _():
+                stage(Square, c - 4)
+
+        for i in range(len(partners)):
+
+            @pl.when(t == 3 * i + 2)
+            def _():
+                if i == 0:
+                    gain_out[0] = gains[...]
+                else:
+                    gain_exchange(i - 1).wait()
+                    gain_out[i] = gain_out[i - 1] + gain_in[i - 1]
+                gain_exchange(i).start()
+
+    last = len(partners) - 1
+    gain_exchange(last).wait()
+    out_gains[...] = gain_out[last] + gain_in[last]
+
+    send_z().wait_send()
+    for kind, base, count in kinds:
+        send_a(kind).wait_send()
+
+    def finish(cls, c):
+        to_near(cls, c).wait_send()
+        to_far(cls, c).wait_send()
+        to_second(cls, c).wait_send()
+        share_second(cls, c).wait_send()
+        share_first(cls, c).wait()
+        pass_on(cls, c).wait()
+        keep(cls, c).wait()
+
+    @pl.loop(0, 4)
+    def _(c):
+        send_e(c).wait_send()
+        finish(Down, c)
+
+    @pl.loop(0, 19)
+    def _(c):
+        send_b(0, 0, c).wait_send()
+        finish(Square, c)
+
+
+def reduce_gradients(group_size, nf_t, na_t, o_t, z_t, dgu, dm, f_cols, e_cols, gains):
+    extra = []
+    mask = 4
+    while mask < group_size:
+        extra.append(mask)
+        mask *= 2
+    n_extra = len(extra)
+    low = jnp.bfloat16
+    tokens = nf_t.shape[1]
+    scratch = [
+        pltpu.VMEM((3, D, tokens), low),
+        pltpu.VMEM((3, D, tokens), low),
+        pltpu.VMEM((4, 352, tokens), low),
+        pltpu.VMEM((4, 352, tokens), low),
+        pltpu.VMEM((19, tokens, BLOCK), low),
+        pltpu.VMEM((19, tokens, BLOCK), low),
+        pltpu.VMEM((4, tokens, BLOCK), low),
+        pltpu.VMEM((4, tokens, BLOCK), low),
+        pltpu.VMEM((19, 2, 2, 256, BLOCK), low),
+        pltpu.VMEM((19, 2, 256, BLOCK), low),
+        pltpu.VMEM((19, 256, BLOCK), low),
+        pltpu.VMEM((19, 128, BLOCK), low),
+        pltpu.VMEM((4, 2, 2, 352, BLOCK), low),
+        pltpu.VMEM((4, 2, 352, BLOCK), low),
+        pltpu.VMEM((4, 352, BLOCK), low),
+        pltpu.VMEM((4, 176, BLOCK), low),
+        pltpu.VMEM((4 + n_extra, 8, D), jnp.float32),
+        pltpu.VMEM((4 + n_extra, 8, D), jnp.float32),
+        pltpu.VMEM((max(n_extra, 1), 19 if n_extra else 1, 128, BLOCK), low),
+        pltpu.VMEM((max(n_extra, 1), 4 if n_extra else 1, 176, BLOCK), low),
+        pltpu.SemaphoreType.DMA((4,)),
+        pltpu.SemaphoreType.DMA((23,)),
+        pltpu.SemaphoreType.DMA((4,)),
+        pltpu.SemaphoreType.DMA((4,)),
+        pltpu.SemaphoreType.DMA((23,)),
+        pltpu.SemaphoreType.DMA((23,)),
+        pltpu.SemaphoreType.DMA((6 + n_extra, 23)),
+        pltpu.SemaphoreType.DMA((6 + n_extra, 23)),
+        pltpu.SemaphoreType.DMA((23,)),
+        pltpu.SemaphoreType.DMA((4 + n_extra,)),
+        pltpu.SemaphoreType.DMA((4 + n_extra,)),
+    ]
+    anywhere = pl.BlockSpec(memory_space=pl.ANY)
+    near_by = pl.BlockSpec(memory_space=pltpu.VMEM)
+    return pl.pallas_call(
+        functools.partial(reduce_kernel, tuple(extra)),
+        out_shape=(
+            jax.ShapeDtypeStruct((2, 19, 256, BLOCK), low),
+            jax.ShapeDtypeStruct((2, 4, 352, BLOCK), low),
+            jax.ShapeDtypeStruct((8, D), jnp.float32),
+        ),
+        in_specs=[anywhere] * 8 + [near_by],
+        out_specs=(anywhere, anywhere, near_by),
+        scratch_shapes=scratch,
+        compiler_params=pltpu.CompilerParams(
+            collective_id=0, has_side_effects=True, vmem_limit_bytes=58 * 2**20
+        ),
+        cost_estimate=pl.CostEstimate(flops=13 * 10**9, bytes_accessed=30 * 10**6, transcendentals=0),
+        name="reduce_gradients",
+    )(nf_t, na_t, o_t, z_t, dgu, dm, f_cols, e_cols, gains)
+
+
+def column_blocks(array):
+    return array.reshape(array.shape[0], -1, BLOCK).transpose(1, 0, 2)
+
+
+def unblock(blocks):
+    blocks = blocks.reshape(-1, *blocks.shape[-2:])
+    return blocks.transpose(1, 0, 2).reshape(blocks.shape[1], -1).astype(jnp.float32)[None]
+
+
+def unpack_gradients(out_sq, out_d, out_gains):
+    start = lax.axis_index("dp") * BLOCK
+    gains = lax.dynamic_slice(out_gains, (0, start), (2, BLOCK))
+    down = out_d.transpose(0, 2, 1, 3).reshape(704, D).astype(jnp.float32)[None]
     return (
-        grad_gain_attn,
-        contract_rows(normed_attn, grad_mixed),
-        contract_rows(attended, grad_attn_out),
-        grad_gain_ffn,
-        contract_rows(normed_ffn, grad_gu),
-        contract_rows(hidden, grad_branch),
+        gains[0:1],
+        unblock(out_sq[:, 13:19]),
+        unblock(out_sq[:, 11:13]),
+        gains[1:2],
+        unblock(out_sq[:, :11]),
+        down,
     )
 
 
 def body(
+    group_size,
     tokens,
     cotangent,
     mem_keys,
@@ -368,16 +709,24 @@
     joined = tuple(
         (jnp.concatenate([item[slot] for item in micro_results], axis=0) for slot in range(2, 10))
     )
-    grad_sums = weight_terms((gain_attn_sum, gain_ffn_sum) + joined)
+    hidden, grad_branch, normed_ffn, grad_gu, attended, grad_attn_out, normed_attn, grad_mixed = joined
+    gains = jnp.zeros((8, D), jnp.float32).at[0].set(gain_attn_sum).at[1].set(gain_ffn_sum)
+    reduced = reduce_gradients(
+        group_size,
+        normed_ffn.T,
+        normed_attn.T,
+        attended.T,
+        hidden.T.reshape(4, 2, 352, -1),
+        column_blocks(grad_gu),
+        column_blocks(grad_mixed),
+        column_blocks(grad_attn_out),
+        column_blocks(grad_branch),
+        gains,
+    )
+    totals = unpack_gradients(*reduced)
     micro_grads = [pick(tick_grads[micro], tick_grads[micro + 1]) for micro in range(MICRO)]
     activations = jnp.concatenate(micro_outputs, axis=0)[None]
     input_grads = jnp.concatenate(micro_grads, axis=0)[None]
-    stacked = tuple((item[None] for item in grad_sums))
-    shards = jax.tree.map(
-        lambda part: part.astype(jnp.float32),
-        lax.psum_scatter(as_sent(stacked), "dp", scatter_dimension=1, tiled=True),
-    )
-    totals = jax.tree.map(lambda part: part.astype(jnp.float32), lax.psum(as_sent(shards), "group"))
     return (
         activations,
         input_grads,
@@ -406,7 +755,7 @@
         P("section", None, None),
     )
     return jax.shard_map(
-        body,
+        functools.partial(body, mesh.shape["group"]),
         mesh=mesh,
         in_specs=placed,
         out_specs=(

time: 1050 us -> 724 us (0.69)
  waiting for transfers between devices: 670 us -> 80.1 us
  Pallas kernels: 0 us -> 249 us
  local copies, waits for them, and re-layouts: 88.3 us -> 175 us
  matrix products: 127 us -> 84.4 us
  between operations: 18.1 us -> 4.72 us
  loops' own time: 23.6 us -> 12.8 us
    reduce_scatter x4 -> x0, waiting for transfers between devices: 428 us -> none  [body(): lax.psum_scatter(as_sent(stacked), 'dp', scatter_dimension=1, tiled=True)]
    pallas_call x0 -> x1, Pallas kernels: none -> 249 us  [reduce_gradients(): pl.pallas_call(functools.partial(reduce_kernel, tuple(extra)), out_shape=...]
    psum x1 -> x0, waiting for transfers between devices: 132 us -> none  [body(): lax.psum(as_sent(shards), 'group')]
    unnamed x9 -> x0, waiting for transfers between devices: 38.8 us -> none
    dot_general x4 -> x0, matrix products: 22.4 us -> none  [contract_rows(): lax.dot_general(left, right, (((0,), (0,)), ((), ())), preferred_element_...]
    convert_element_type x0 -> x6, local copies, waits for them, and re-layouts: none -> 20.1 us  [the longest x4 12 us: unblock(): blocks.transpose(1, 0, 2).reshape(blocks.shape[1], -1).astype(jnp.float32)]
    reshape x0 -> x4, local copies, waits for them, and re-layouts: none -> 16 us  [column_blocks(): return array.reshape(array.shape[0], -1, BLOCK).transpose(1, 0, 2)]
    dot_general x8, matrix products: 42.7 us -> 30 us  [contract_cols(): lax.dot_general(left, right, (((1,), (1,)), ((), ())), preferred_element_...]
  transfers between devices with their start and end apart: 11 -> 4, of which waited for: 9 -> 2; matrix products, arithmetic and copies ran while one was open for 8% -> 9% of each run, Pallas kernels for 0% -> 0%
where the time goes in v1:
time: 724 us; the launch traced here: 716 us
  Pallas kernels  249 us (34%)
  local copies, waits for them, and re-layouts  175 us (24%)
  other arithmetic  104 us (14%)
  matrix products  84.4 us (12%)
  waiting for transfers between devices  80.1 us (11%)
  loops' own time  12.8 us (2%)
    pallas_call x1, Pallas kernels, reduce_gradients(): pl.pallas_call(functools.partial(reduce_kernel, tuple(extra)), out_shape=...  249 us
    ppermute x4, waiting for transfers between devices, from_behind(): return lax.ppermute(block, axis, route)  80.1 us
    select_n x18, other arithmetic, pick(): jnp.where(upper_section, upper_leaf, lower_leaf)  38.5 us
    another operation x40, local copies, waits for them, and re-layouts  36.7 us
    dot_general x8, matrix products, contract_cols(): lax.dot_general(left, right, (((1,), (1,)), ((), ())), preferred_element_...  30 us
    unnamed x187, local copies, waits for them, and re-layouts  26 us
    reshape x4, local copies, waits for them, and re-layouts, column_blocks(): return array.reshape(array.shape[0], -1, BLOCK).transpose(1, 0, 2)  16 us
    cond x8, local copies, waits for them, and re-layouts, body(): lax.cond(busy, forward_active, forward_spare, (layer_input, memory))  14.9 us
  transfers between devices with their start and end apart: 4, of which 2 were waited for; matrix products, arithmetic and copies ran while one was open for 9% of the time, Pallas kernels for 0%

profile of v1, /device:TPU:0, one launch (start us, length us, event | category | flops | bytes accessed | tf_op | source)
XLA Modules:
  0.0 716.0 jit_solution(18334646921873908772)
XLA Ops:
  6.1 2.8 gather_fusion.1
  9.8 2.8 gather_fusion
  16.4 45.7 %conditional.4 = (f32[256,1]{0,1:T(1,128)S(1)}, bf16[256,1024]{1,0:T(8,128)(2,1)}, bf16[1,256,8,128]{3,1,2,0:T(8,128)(2,1)}, bf16[1,256,8,128]{3,1,2,0:T(8,128)(...) conditional(s32[]{:T(128)} %convert_element_type.550, () %tuple.77, ...), branch_computations={%region_0.0_spmd, %region_1.9_spmd} | conditional | flops 6999523840 | bytes 168662144 | solution.py:661
  18.0 4.8 convolution_bitcast_fusion
  41.3 2.8 multiply_reduce_fusion
  46.4 6.1 fusion.239
  52.6 4.6 fusion
  57.2 3.4 fusion.3
  68.0 8.9 %copy.336 = bf16[3072,1024]{1,0:T(8,128)(2,1)} copy(bf16[3072,1024]{0,1:T(8,128)(2,1)} %bitcast.547) | data formatting | bytes 12582912 | tf_op jit(solution)/shard_map/cond/branch_1_fun/dot_general | solution.py:81
  80.2 2.5 copy.229
  89.0 4.8 convolution_bitcast_fusion.8
  101.8 6.8 fusion.206
  108.6 4.6 fusion.142
  113.2 4.6 fusion.152
  125.0 7.8 %conditional.6 = (f32[1024]{0:T(1024)S(1)}, f32[1024]{0:T(1024)S(1)}, bf16[256,2816]{1,0:T(8,128)(2,1)S(1)}, bf16[256,5632]{1,0:T(8,128)(2,1)}, bf16[256,3072]{0...) conditional(s32[]{:T(128)} %convert_element_type.551, () %tuple.81, ...), branch_computations={%region_22.24_spmd, %region_23.31_spmd} | conditional | flops 7488881664 | bytes 306992928 | solution.py:695
  136.1 20.4 %conditional.5 = (f32[256,1]{0,1:T(1,128)S(1)}, bf16[256,1024]{1,0:T(8,128)(2,1)}, bf16[1,256,8,128]{3,1,2,0:T(8,128)(2,1)}, bf16[1,256,8,128]{3,1,2,0:T(8,128)(...) conditional(s32[]{:T(128)} %convert_element_type.551, () %tuple.79, ...), branch_computations={%region_14.16_spmd, %region_15.23_spmd} | conditional | flops 6999523840 | bytes 193303840 | solution.py:661
  142.4 3.2 broadcast.773
  156.5 4.1 broadcast_select_fusion.13
  160.7 43.1 %collective-permute-done.2 = bf16[256,1024]{0,1:T(8,128)(2,1)} collective-permute-done((bf16[256,1024]{0,1:T(8,128)(2,1)}, bf16[256,1024]{0,1:T(8,128)(2,1)}, u32[]{:S(2)}, u32[]{:S(2)}) %collective-permute-start.2) | collective-permute-done | bytes 524320 | tf_op jit(solution)/shard_map/ppermute | solution.py:27
  203.8 5.4 fusion.141
  210.9 3.2 fusion.178
  215.3 3.1 broadcast_select_fusion.26
  233.3 2.9 fusion.164
  250.9 37.0 %collective-permute-done.3 = bf16[256,1024]{0,1:T(8,128)(2,1)} collective-permute-done((bf16[256,1024]{0,1:T(8,128)(2,1)}, bf16[256,1024]{0,1:T(8,128)(2,1)}, u32[]{:S(2)}, u32[]{:S(2)}) %collective-permute-start.3) | collective-permute-done | bytes 524320 | tf_op jit(solution)/shard_map/ppermute | solution.py:27
  290.1 78.4 %conditional.7 = (f32[1024]{0:T(1024)S(1)}, f32[1024]{0:T(1024)S(1)}, bf16[256,2816]{1,0:T(8,128)(2,1)S(1)}, bf16[256,5632]{1,0:T(8,128)(2,1)}, bf16[256,3072]{0...) conditional(s32[]{:T(128)} %convert_element_type.550, () %tuple.83, ...), branch_computations={%region_34.36_spmd, %region_35.43_spmd} | conditional | flops 7488881664 | bytes 316897152 | solution.py:695
  296.3 7.8 %select_n.464 = f32[256,5632]{1,0:T(8,128)} select(pred[256,5632]{1,0:T(8,128)(4,1)S(1)} %get-tuple-element.614, f32[256,5632]{1,0:T(8,128)} %get-tuple-element.615, f32[256,5632]{1,0:T(8,128)} %get-tuple-element.616) | non-fusion elementwise | flops 1441792 | bytes 18743296 | tf_op jit(solution)/shard_map/jit(_where)/select_n | solution.py:638
  309.8 2.6 broadcast_select_fusion.7
  312.5 7.0 fusion.102
  322.1 6.3 multiply_reduce_fusion.7
  328.4 3.3 fusion.219
  335.4 3.1 fusion.120
  342.1 2.7 multiply_reduce_fusion.6
  355.1 3.1 select_n.470
  371.9 4.8 copy.272
  376.7 2.6 broadcast_select_fusion.12
  379.3 2.9 pad_maximum_fusion.8
  382.2 8.4 %copy.273 = bf16[512,5632]{0,1:T(8,128)(2,1)} copy(bf16[512,5632]{1,0:T(8,128)(2,1)} %pad_maximum_fusion.8) | data formatting | bytes 11534336 | tf_op jit(solution)/shard_map/concatenate | solution.py:710
  390.6 8.5 %copy.274 = bf16[512,22,256]{2,0,1:T(8,128)(2,1)} copy(bf16[512,22,256]{0,2,1:T(8,128)(2,1)} %bitcast.523) | data formatting | bytes 11534336 | tf_op jit(solution)/shard_map/reshape | solution.py:574
  402.7 4.8 copy.275
  420.3 248.8 %reduce_gradients.1 = (bf16[2,19,256,256]{3,2,1,0:T(8,128)(2,1)}, bf16[2,4,352,256]{3,2,1,0:T(8,128)(2,1)}, f32[8,1024]{1,0:T(8,128)}) custom-call(bf16[1024,512]{1,0:T(8,128)(2,1)} %maximum_bitcast_fusion.3.refs_0_, bf16[1024,512]{1,0:T(8,128)(2,1)} %maximum_bitcast_fusion.4.refs_1_, bf16[1024,512]{1,0:T(8,128)(2,1)} %maximum_bitcast_fusion.5.refs_2_, ...), custom_call_target="tpu_custom_call" | custom-call | flops 12999999488 | bytes 30000000 | tf_op jit(solution)/shard_map/reduce_gradients/pallas_call | solution.py:555
  671.7 3.8 slice.313
  678.9 3.5 copy.284
  682.4 3.5 copy.290
  688.3 5.0 bitcast_convert_fusion
  693.3 6.2 copy.286
  699.6 6.3 copy.291
  706.2 3.5 copy.287
  709.7 4.7 reshape.1553
  (515 shorter events, 183.9 us)
Async XLA Ops:
  0.6 5.4 copy-start
  16.8 6.0 copy-start.24
  17.0 5.8 copy-start.149
  35.8 10.7 %slice-start.6 = ((s8[11534336]{0:T(1024)(128)(4,1)}), s8[4194304]{0:T(1024)(128)(4,1)S(1)}, s32[]{:S(2)}) async-start(s8[11534336]{0:T(1024)(128)(4,1)} %bitcast.511), calls=%async_computation.6 | async-start | bytes 8388608 | tf_op jit(solution)/shard_map/cond
  37.5 8.9 %slice-start.7 = ((s8[11534336]{0:T(1024)(128)(4,1)}), s8[4194304]{0:T(1024)(128)(4,1)S(1)}, s32[]{:S(2)}) async-start(s8[11534336]{0:T(1024)(128)(4,1)} %bitcast.511), calls=%async_computation.7 | async-start | bytes 8388608 | tf_op jit(solution)/shard_map/cond
  40.1 6.3 slice-start.8
  44.0 8.5 %copy-start.155 = (f32[256]{0:T(256)}, f32[256]{0:T(256)S(1)}, u32[]{:S(2)}) copy-start(f32[256]{0:T(256)S(1)} %add_rsqrt_fusion) | copy-start | bytes 3076 | tf_op jit(solution)/shard_map/cond
  44.0 13.2 %slice-start.26 = ((s8[5767168]{0:T(1024)(128)(4,1)}), s8[4194304]{0:T(1024)(128)(4,1)S(1)}, s32[]{:S(2)}) async-start(s8[5767168]{0:T(1024)(128)(4,1)} %bitcast.623), calls=%async_computation.26 | async-start | bytes 8388608 | tf_op jit(solution)/shard_map/cond
  46.4 10.8 %slice-start.27 = ((s8[5767168]{0:T(1024)(128)(4,1)}), s8[1572864]{0:T(1024)(128)(4,1)S(1)}, s32[]{:S(2)}) async-start(s8[5767168]{0:T(1024)(128)(4,1)} %bitcast.623), calls=%async_computation.27 | async-start | bytes 3145728 | tf_op jit(solution)/shard_map/cond
  62.0 62.9 %copy-start.151 = (f32[256,1]{0,1:T(1,128)}, f32[256,1]{0,1:T(1,128)S(1)}, u32[]{:S(2)}) copy-start(f32[256,1]{0,1:T(1,128)S(1)} %get-tuple-element.710) | copy-start | bytes 3076
  62.0 62.9 %copy-start.157 = (f32[256,1]{0,1:T(1,128)}, f32[256,1]{0,1:T(1,128)S(1)}, u32[]{:S(2)}) copy-start(f32[256,1]{0,1:T(1,128)S(1)} %get-tuple-element.706) | copy-start | bytes 3076
  62.1 26.5 %collective-permute-start = (bf16[256,1024]{0,1:T(8,128)(2,1)}, bf16[256,1024]{0,1:T(8,128)(2,1)}, u32[]{:S(2)}, u32[]{:S(2)}) collective-permute-start(bf16[256,1024]{0,1:T(8,128)(2,1)} %get-tuple-element.1030), channel_id=1, source_target_pairs={{0,16},{1,17},{2,18},{3,19},{4,20},{5,21},{6,22},{7,23},{8,24},{9,... | collective-permute-start | bytes 1572872 | tf_op jit(solution)/shard_map/ppermute | solution.py:27
  64.2 24.6 %copy-start.130 = (f32[1024]{0:T(1024)}, f32[1024]{0:T(1024)S(1)}, u32[]{:S(2)}) copy-start(f32[1024]{0:T(1024)S(1)} %convert_element_type.553) | copy-start | bytes 12292
  68.0 20.5 %copy-start.56 = (bf16[256,1024]{0,1:T(8,128)(2,1)}, bf16[256,1024]{0,1:T(8,128)(2,1)S(1)}, u32[]{:S(2)}) copy-start(bf16[256,1024]{0,1:T(8,128)(2,1)S(1)} %copy.378) | copy-start | bytes 1572868
  88.8 36.2 %copy-start.136 = (f32[256]{0:T(256)}, f32[256]{0:T(256)S(1)}, u32[]{:S(2)}) copy-start(f32[256]{0:T(256)S(1)} %add_rsqrt_fusion.5) | copy-start | bytes 3076
  95.5 6.3 slice-start
  96.4 5.4 slice-start.1
  100.8 24.2 %copy-start.138 = (f32[256]{0:T(256)}, f32[256]{0:T(256)S(1)}, u32[]{:S(2)}) copy-start(f32[256]{0:T(256)S(1)} %add_rsqrt_fusion.4) | copy-start | bytes 3076
  100.8 12.5 %slice-start.24 = ((s8[5767168]{0:T(1024)(128)(4,1)}), s8[4194304]{0:T(1024)(128)(4,1)S(1)}, s32[]{:S(2)}) async-start(s8[5767168]{0:T(1024)(128)(4,1)} %bitcast.620), calls=%async_computation.24 | async-start | bytes 8388608
  101.8 11.4 %slice-start.25 = ((s8[5767168]{0:T(1024)(128)(4,1)}), s8[1572864]{0:T(1024)(128)(4,1)S(1)}, s32[]{:S(2)}) async-start(s8[5767168]{0:T(1024)(128)(4,1)} %bitcast.620), calls=%async_computation.25 | async-start | bytes 3145728
  117.9 16.2 %collective-permute-start.1 = (bf16[256,1024]{0,1:T(8,128)(2,1)}, bf16[256,1024]{0,1:T(8,128)(2,1)}, u32[]{:S(2)}, u32[]{:S(2)}) collective-permute-start(bf16[256,1024]{0,1:T(8,128)(2,1)} %fusion.152), channel_id=1, source_target_pairs={{0,16},{1,17},{2,18},{3,19},{4,20},{5,21},{6,22},{7,23},{8,24},{9,... | collective-permute-start | bytes 1572872 | tf_op jit(solution)/shard_map/ppermute | solution.py:27
  132.8 71.0 %collective-permute-start.2 = (bf16[256,1024]{0,1:T(8,128)(2,1)}, bf16[256,1024]{0,1:T(8,128)(2,1)}, u32[]{:S(2)}, u32[]{:S(2)}) collective-permute-start(bf16[256,1024]{0,1:T(8,128)(2,1)} %get-tuple-element.1035), channel_id=1, source_target_pairs={{16,0},{17,1},{18,2},{19,3},{20,4},{21,5},{22,6},{23,7},{24,8},{25... | collective-permute-start | bytes 1572872 | tf_op jit(solution)/shard_map/ppermute | solution.py:27
  156.5 47.3 %copy-start.67 = (bf16[256,1024]{0,1:T(8,128)(2,1)S(1)}, bf16[256,1024]{0,1:T(8,128)(2,1)}, u32[]{:S(2)}) copy-start(bf16[256,1024]{0,1:T(8,128)(2,1)} %copy.379) | copy-start | bytes 1572868
  160.6 50.3 %slice-start.3 = ((s8[11534336]{0:T(1024)(128)(4,1)}), s8[4194304]{0:T(1024)(128)(4,1)S(1)}, s32[]{:S(2)}) async-start(s8[11534336]{0:T(1024)(128)(4,1)} %bitcast.509), calls=%async_computation.3 | async-start | bytes 8388608
  160.7 50.2 %slice-start.4 = ((s8[11534336]{0:T(1024)(128)(4,1)}), s8[4194304]{0:T(1024)(128)(4,1)S(1)}, s32[]{:S(2)}) async-start(s8[11534336]{0:T(1024)(128)(4,1)} %bitcast.509), calls=%async_computation.4 | async-start | bytes 8388608
  160.7 50.2 %slice-start.5 = ((s8[11534336]{0:T(1024)(128)(4,1)}), s8[3145728]{0:T(1024)(128)(4,1)S(1)}, s32[]{:S(2)}) async-start(s8[11534336]{0:T(1024)(128)(4,1)} %bitcast.509), calls=%async_computation.5 | async-start | bytes 6291456
  231.0 5.2 copy-start.47
  237.6 50.3 %collective-permute-start.3 = (bf16[256,1024]{0,1:T(8,128)(2,1)}, bf16[256,1024]{0,1:T(8,128)(2,1)}, u32[]{:S(2)}, u32[]{:S(2)}) collective-permute-start(bf16[256,1024]{0,1:T(8,128)(2,1)} %get-tuple-element.1078), channel_id=1, source_target_pairs={{16,0},{17,1},{18,2},{19,3},{20,4},{21,5},{22,6},{23,7},{24,8},{25... | collective-permute-start | bytes 1572872 | tf_op jit(solution)/shard_map/ppermute | solution.py:27
  245.5 44.6 %copy-start.17 = (pred[256,5632]{1,0:T(8,128)(4,1)S(1)}, pred[256,5632]{1,0:T(8,128)(4,1)}, u32[]{:S(2)}) copy-start(pred[256,5632]{1,0:T(8,128)(4,1)} %select_n.560) | copy-start | bytes 4325380
  245.5 44.6 %copy-start.134 = (pred[1,8,256]{2,1,0:T(8,128)(4,1)S(1)}, pred[1,8,256]{2,1,0:T(8,128)(4,1)}, u32[]{:S(2)}) copy-start(pred[1,8,256]{2,1,0:T(8,128)(4,1)} %copy-done.133) | copy-start | bytes 6148
  245.5 44.6 %copy-start.137 = (f32[256]{0:T(256)S(1)}, f32[256]{0:T(256)}, u32[]{:S(2)}) copy-start(f32[256]{0:T(256)} %copy-done.136) | copy-start | bytes 3076
  245.5 44.6 %copy-start.139 = (f32[256]{0:T(256)S(1)}, f32[256]{0:T(256)}, u32[]{:S(2)}) copy-start(f32[256]{0:T(256)} %copy-done.138) | copy-start | bytes 3076
  245.5 44.6 %copy-start.162 = (pred[256,1]{0,1:T(4,128)(4,1)S(1)}, pred[256,1]{0,1:T(4,128)(4,1)}, u32[]{:S(2)}) copy-start(pred[256,1]{0,1:T(4,128)(4,1)} %copy-done.161) | copy-start | bytes 772
  290.6 13.6 %copy-start.33 = (bf16[256,1024]{1,0:T(8,128)(2,1)}, bf16[256,1024]{1,0:T(8,128)(2,1)S(1)}, u32[]{:S(2)}) copy-start(bf16[256,1024]{1,0:T(8,128)(2,1)S(1)} %get-tuple-element.635) | copy-start | bytes 1572868 | tf_op jit(solution)/shard_map/cond
  304.2 5.6 copy-start.34
  309.8 9.7 %copy-start.21 = (f32[256,1024]{1,0:T(8,128)}, f32[256,1024]{1,0:T(8,128)S(1)}, u32[]{:S(2)}) copy-start(f32[256,1024]{1,0:T(8,128)S(1)} %copy.252) | copy-start | bytes 3145732 | tf_op jit(solution)/shard_map/cond
  309.8 11.5 %slice-start.15 = ((s8[11534336]{0:T(1024)(128)(4,1)}), s8[4194304]{0:T(1024)(128)(4,1)S(1)}, s32[]{:S(2)}) async-start(s8[11534336]{0:T(1024)(128)(4,1)} %bitcast.517), calls=%async_computation.15 | async-start | bytes 8388608 | tf_op jit(solution)/shard_map/cond
  312.5 7.1 copy-start.91
  312.5 8.9 %slice-start.16 = ((s8[11534336]{0:T(1024)(128)(4,1)}), s8[4194304]{0:T(1024)(128)(4,1)S(1)}, s32[]{:S(2)}) async-start(s8[11534336]{0:T(1024)(128)(4,1)} %bitcast.517), calls=%async_computation.16 | async-start | bytes 8388608 | tf_op jit(solution)/shard_map/cond
  312.5 8.9 %slice-start.17 = ((s8[11534336]{0:T(1024)(128)(4,1)}), s8[3145728]{0:T(1024)(128)(4,1)S(1)}, s32[]{:S(2)}) async-start(s8[11534336]{0:T(1024)(128)(4,1)} %bitcast.517), calls=%async_computation.17 | async-start | bytes 6291456 | tf_op jit(solution)/shard_map/cond
  335.4 6.5 copy-start.37
  335.4 6.5 copy-start.65
  350.1 5.0 copy-start.50
  362.0 5.3 copy-start.92
  363.2 5.1 copy-start.53
  390.6 8.5 %copy-start.48 = (bf16[1,256,3,8,128]{1,4,3,2,0:T(8,128)(2,1)S(1)}, bf16[1,256,3,8,128]{1,4,3,2,0:T(8,128)(2,1)}, u32[]{:S(2)}) copy-start(bf16[1,256,3,8,128]{1,4,3,2,0:T(8,128)(2,1)} %copy-done.47) | copy-start | bytes 4718596
  699.6 6.3 copy-start.111
  706.2 9.6 %copy-start.1 = (bf16[2,256,1024]{2,1,0:T(8,128)(2,1)S(1)}, bf16[2,256,1024]{2,1,0:T(8,128)(2,1)}, u32[]{:S(2)}) copy-start(bf16[2,256,1024]{2,1,0:T(8,128)(2,1)} %param.29) | copy-start | bytes 3145732
  (100 other events, 264.9 us)

commit v2 on v1

v2 whole, which is shorter than its diff:
```python
import functools

import jax
import jax.numpy as jnp
import numpy as np
from jax import lax
from jax.experimental import pallas as pl
from jax.experimental.pallas import tpu as pltpu
from jax.sharding import PartitionSpec as P

D = 1024
HEADS = 8
HEAD_DIM = 128
FF = 2816
SEG = 256
TOPM = 128
MICRO = 2
EPS = 1e-05
NEG = -1e30
MESH = pl.DeviceIdType.MESH
BLOCK = 256
LAG = 2


def flip(value, mask):
    return value + mask * (1 - 2 * ((value // mask) % 2))


def summed(left, right):
    return (left.astype(jnp.float32) + right.astype(jnp.float32)).astype(jnp.bfloat16)


def reduce_kernel(extra, *refs):
    n_extra = len(extra)
    (nf_t, na_t, o_t, z_t, dgu, dm, f_cols, e_cols, gains) = refs[:9]
    (out_sq, out_d, out_gains) = refs[9:12]
    refs = refs[12:]
    (a_own, a_in, z_own, z_in, b_own, b_in, e_own, e_in) = refs[:8]
    (g_sq, q0, q1, q2, g_d, d0, d1, d2, gain_out, gain_in) = refs[8:18]
    refs = refs[18:]
    x_sq, x_d = refs[:2]
    (sem_load, sem_bload, sem_asend, sem_arecv, sem_bsend, sem_brecv) = refs[2:8]
    (sem_send, sem_recv, sem_copy, gain_send, gain_recv) = refs[8:13]

    section, dpi, group = (lax.axis_index(name) for name in ("section", "dp", "group"))
    mask1 = 1 + section
    mask2 = 2 - section
    half = (group // mask1) % 2
    low2 = (group // mask2) % 2
    bit0 = dpi % 2
    bit1 = (dpi // 2) % 2
    first = (section, dpi, flip(group, mask1))
    second = (section, dpi, flip(group, mask2))
    near = (section, flip(dpi, 1), group)
    far = (section, flip(dpi, 2), group)
    others = [(section, dpi, flip(group, mask)) for mask in extra]
    partners = [first, second, near, far] + others

    barrier = pltpu.get_barrier_semaphore()
    for partner in partners:
        pl.semaphore_signal(barrier, inc=1, device_id=partner, device_id_type=MESH)
    pl.semaphore_wait(barrier, len(partners))

    def remote(src, dst, send, recv, device):
        return pltpu.make_async_remote_copy(
            src_ref=src, dst_ref=dst, send_sem=send, recv_sem=recv, device_id=device, device_id_type=MESH
        )

    def load_a(slot):
        src = (nf_t, o_t, na_t)[slot]
        return pltpu.make_async_copy(src, a_own.at[slot], sem_load.at[slot])

    def load_z():
        return pltpu.make_async_copy(z_t.at[pl.ds(0, 4), half], z_own, sem_load.at[3])

    def b_src(index, part):
        if index[0] == 0:
            return dgu.at[part * 11 + index[1]]
        if index[0] == 1:
            return f_cols.at[part * 2 + index[1]]
        return dm.at[part * 6 + index[1]]

    def load_b(kind, i, slot):
        return pltpu.make_async_copy(b_src((kind, i), half), b_own.at[slot], sem_bload.at[slot])

    def load_e(k):
        return pltpu.make_async_copy(e_cols.at[k], e_own.at[k], sem_bload.at[19 + k])

    def send_a(slot):
        src = (nf_t, o_t, na_t)[slot]
        return remote(src, a_in.at[slot], sem_asend.at[slot], sem_arecv.at[slot], first)

    def send_z():
        return remote(z_t.at[pl.ds(0, 4), 1 - half], z_in, sem_asend.at[3], sem_arecv.at[3], first)

    def send_b(kind, i, slot):
        return remote(b_src((kind, i), 1 - half), b_in.at[slot], sem_bsend.at[slot], sem_brecv.at[slot], first)

    def send_e(k):
        return remote(e_cols.at[k], e_in.at[k], sem_bsend.at[19 + k], sem_brecv.at[19 + k], first)

    kinds = ((0, 0, 11), (1, 11, 2), (2, 13, 6))
    load_z().start()
    send_z().start()

    @pl.loop(0, 4)
    def _(k):
        load_e(k).start()
        send_e(k).start()

    for kind, base, count in kinds:
        load_a(kind).start()
        send_a(kind).start()

        @pl.loop(0, count)
        def _(i):
            load_b(kind, i, base + i).start()
            send_b(kind, i, base + i).start()

    class Square:
        base, rows = 4, 256
        partial, recv0, recv1, recv2, xs, out = g_sq, q0, q1, q2, x_sq, out_sq

    class Down:
        base, rows = 0, 352
        partial, recv0, recv1, recv2, xs, out = g_d, d0, d1, d2, x_d, out_d

    def to_near(cls, c):
        k = cls.base + c
        return remote(cls.partial.at[c, pl.ds(0, 2), 1 - bit0], cls.recv0.at[c], sem_send.at[0, k], sem_recv.at[0, k], near)

    def to_far(cls, c):
        k = cls.base + c
        return remote(cls.recv0.at[c, 1 - bit1], cls.recv1.at[c], sem_send.at[1, k], sem_recv.at[1, k], far)

    def rows_at(cls, part):
        size = cls.rows // 2
        return pl.ds(pl.multiple_of(part * size, 16), size)

    def to_second(cls, c):
        k = cls.base + c
        return remote(cls.recv1.at[c, rows_at(cls, 1 - low2)], cls.recv2.at[c], sem_send.at[2, k], sem_recv.at[2, k], second)

    def to_extra(cls, c, i):
        k = cls.base + c
        src = cls.recv2.at[c] if i == 0 else cls.xs.at[i - 1, c]
        return remote(src, cls.xs.at[i, c], sem_send.at[6 + i, k], sem_recv.at[6 + i, k], others[i])

    def final(cls, c):
        return cls.recv2.at[c] if n_extra == 0 else cls.xs.at[n_extra - 1, c]

    def share_second(cls, c):
        k = cls.base + c
        return remote(final(cls, c), cls.out.at[half, c, rows_at(cls, low2)], sem_send.at[3, k], sem_recv.at[3, k], second)

    def share_first(cls, c):
        k = cls.base + c
        return remote(final(cls, c), cls.out.at[half, c, rows_at(cls, low2)], sem_send.at[4, k], sem_recv.at[4, k], first)

    def pass_on(cls, c):
        k = cls.base + c
        block = cls.out.at[half, c, rows_at(cls, 1 - low2)]
        return remote(block, block, sem_send.at[5, k], sem_recv.at[5, k], first)

    def keep(cls, c):
        return pltpu.make_async_copy(final(cls, c), cls.out.at[half, c, rows_at(cls, low2)], sem_copy.at[cls.base + c])

    def multiply(left, right, left2, right2):
        total = jnp.dot(left, right, preferred_element_type=jnp.float32)
        total += jnp.dot(left2, right2, preferred_element_type=jnp.float32)
        return total.astype(jnp.bfloat16)

    def partial_square(c):
        for kind, base, count in kinds:

            @pl.when(c == base)
            def _():
                load_a(kind).wait()
                send_a(kind).wait_recv()

        load_b(0, 0, c).wait()
        send_b(0, 0, c).wait_recv()
        for kind, base, count in kinds:

            @pl.when((c >= base) & (c < base + count))
            def _():
                for j in range(4):
                    rows = pl.ds(j * 256, 256)
                    g_sq[c, j // 2, j % 2] = multiply(
                        a_own[kind, rows, :], b_own[c], a_in[kind, rows, :], b_in[c]
                    )

        to_near(Square, c).start()

    def partial_down(c):
        @pl.when(c == 0)
        def _():
            load_z().wait()
            send_z().wait_recv()

        load_e(c).wait()
        send_e(c).wait_recv()
        for j in range(4):
            g_d[c, j // 2, j % 2] = multiply(z_own[j], e_own[c], z_in[j], e_in[c])
        to_near(Down, c).start()

    def stage_near(cls, c):
        to_near(cls, c).wait_recv()
        for i in range(2):
            cls.recv0[c, i] = summed(cls.partial[c, i, bit0], cls.recv0[c, i])
        to_far(cls, c).start()

    def stage_far(cls, c):
        to_far(cls, c).wait_recv()
        cls.recv1[c] = summed(cls.recv0[c, bit1], cls.recv1[c])
        to_second(cls, c).start()

    def share(cls, c):
        share_second(cls, c).start()
        share_first(cls, c).start()
        keep(cls, c).start()

    def stage_second(cls, c):
        to_second(cls, c).wait_recv()
        cls.recv2[c] = summed(cls.recv1[c, rows_at(cls, low2)], cls.recv2[c])
        if n_extra:
            to_extra(cls, c, 0).start()
        else:
            share(cls, c)

    def stage_extra(cls, c, i):
        to_extra(cls, c, i).wait()
        mine = cls.recv2[c] if i == 0 else cls.xs[i - 1, c]
        cls.xs[i, c] = summed(mine, cls.xs[i, c])
        if i + 1 < n_extra:
            to_extra(cls, c, i + 1).start()
        else:
            share(cls, c)

    def stage_pass(cls, c):
        share_second(cls, c).wait_recv()
        pass_on(cls, c).start()

    def partial(cls, c):
        (partial_square if cls is Square else partial_down)(c)

    stages = [partial, stage_near, stage_far, stage_second]
    stages += [functools.partial(lambda i, cls, c: stage_extra(cls, c, i), i) for i in range(n_extra)]
    stages += [stage_pass]

    def gain_exchange(i):
        return remote(gain_out.at[i], gain_in.at[i], gain_send.at[i], gain_recv.at[i], partners[i])

    steps = 23 + LAG * (len(stages) - 1)

    @pl.loop(0, steps)
    def _(t):
        for i, stage in enumerate(stages):
            c = t - LAG * i

            @pl.when((c >= 0) & (c < 4))
            def _():
                stage(Down, c)

            @pl.when((c >= 4) & (c < 23))
            def _():
                stage(Square, c - 4)

        for i in range(len(partners)):

            @pl.when(t == 3 * i + 2)
            def _():
                if i == 0:
                    gain_out[0] = gains[...]
                else:
                    gain_exchange(i - 1).wait()
                    gain_out[i] = gain_out[i - 1] + gain_in[i - 1]
                gain_exchange(i).start()

    last = len(partners) - 1
    gain_exchange(last).wait()
    out_gains[...] = gain_out[last] + gain_in[last]

    send_z().wait_send()
    for kind, base, count in kinds:
        send_a(kind).wait_send()

    def finish(cls, c):
        to_near(cls, c).wait_send()
        to_far(cls, c).wait_send()
        to_second(cls, c).wait_send()
        share_second(cls, c).wait_send()
        share_first(cls, c).wait()
        pass_on(cls, c).wait()
        keep(cls, c).wait()

    @pl.loop(0, 4)
    def _(c):
        send_e(c).wait_send()
        finish(Down, c)

    @pl.loop(0, 19)
    def _(c):
        send_b(0, 0, c).wait_send()
        finish(Square, c)


def reduce_gradients(group_size, nf_t, na_t, o_t, z_t, dgu, dm, f_cols, e_cols, gains):
    extra = []
    mask = 4
    while mask < group_size:
        extra.append(mask)
        mask *= 2
    n_extra = len(extra)
    low = jnp.bfloat16
    tokens = nf_t.shape[1]
    scratch = [
        pltpu.VMEM((3, D, tokens), low),
        pltpu.VMEM((3, D, tokens), low),
        pltpu.VMEM((4, 352, tokens), low),
        pltpu.VMEM((4, 352, tokens), low),
        pltpu.VMEM((19, tokens, BLOCK), low),
        pltpu.VMEM((19, tokens, BLOCK), low),
        pltpu.VMEM((4, tokens, BLOCK), low),
        pltpu.VMEM((4, tokens, BLOCK), low),
        pltpu.VMEM((19, 2, 2, 256, BLOCK), low),
        pltpu.VMEM((19, 2, 256, BLOCK), low),
        pltpu.VMEM((19, 256, BLOCK), low),
        pltpu.VMEM((19, 128, BLOCK), low),
        pltpu.VMEM((4, 2, 2, 352, BLOCK), low),
        pltpu.VMEM((4, 2, 352, BLOCK), low),
        pltpu.VMEM((4, 352, BLOCK), low),
        pltpu.VMEM((4, 176, BLOCK), low),
        pltpu.VMEM((4 + n_extra, 8, D), jnp.float32),
        pltpu.VMEM((4 + n_extra, 8, D), jnp.float32),
        pltpu.VMEM((max(n_extra, 1), 19 if n_extra else 1, 128, BLOCK), low),
        pltpu.VMEM((max(n_extra, 1), 4 if n_extra else 1, 176, BLOCK), low),
        pltpu.SemaphoreType.DMA((4,)),
        pltpu.SemaphoreType.DMA((23,)),
        pltpu.SemaphoreType.DMA((4,)),
        pltpu.SemaphoreType.DMA((4,)),
        pltpu.SemaphoreType.DMA((23,)),
        pltpu.SemaphoreType.DMA((23,)),
        pltpu.SemaphoreType.DMA((6 + n_extra, 23)),
        pltpu.SemaphoreType.DMA((6 + n_extra, 23)),
        pltpu.SemaphoreType.DMA((23,)),
        pltpu.SemaphoreType.DMA((4 + n_extra,)),
        pltpu.SemaphoreType.DMA((4 + n_extra,)),
    ]
    anywhere = pl.BlockSpec(memory_space=pl.ANY)
    near_by = pl.BlockSpec(memory_space=pltpu.VMEM)
    return pl.pallas_call(
        functools.partial(reduce_kernel, tuple(extra)),
        out_shape=(
            jax.ShapeDtypeStruct((2, 19, 256, BLOCK), low),
            jax.ShapeDtypeStruct((2, 4, 352, BLOCK), low),
            jax.ShapeDtypeStruct((8, D), jnp.float32),
        ),
        in_specs=[anywhere] * 8 + [near_by],
        out_specs=(anywhere, anywhere, near_by),
        scratch_shapes=scratch,
        compiler_params=pltpu.CompilerParams(
            collective_id=0, has_side_effects=True, vmem_limit_bytes=58 * 2**20
        ),
        cost_estimate=pl.CostEstimate(flops=13 * 10**9, bytes_accessed=30 * 10**6, transcendentals=0),
        name="reduce_gradients",
    )(nf_t, na_t, o_t, z_t, dgu, dm, f_cols, e_cols, gains)


def to_f32(value):
    return value.astype(jnp.float32)


def to_low(value):
    return value.astype(jnp.bfloat16)


def by_rows(left, right):
    return lax.dot_general(left, right, (((1,), (1,)), ((), ())), preferred_element_type=jnp.float32)


def by_tokens(left, right):
    return lax.dot_general(left, right, (((0,), (0,)), ((), ())), preferred_element_type=jnp.float32)


def times(left, right):
    return jnp.dot(left, right, preferred_element_type=jnp.float32)


def cols(index, size=BLOCK, base=0):
    return pl.ds(pl.multiple_of(base + index * size, 128), size)


def inverse_rms(values):
    return lax.rsqrt(jnp.mean(values * values, axis=-1, keepdims=True) + EPS)


def layer_kernel(*refs):
    (tokens, cotangent, mem_k, mem_v, index, bias, cosine, sine, gain_a, gain_f) = refs[:10]
    (w_qkv_hbm, w_o_hbm, w_gu_hbm, w_d_hbm) = refs[10:14]
    (act, igrad, na_t, nf_t, o_t, z_t, dgu, dm, f_cols, e_cols, gains) = refs[14:25]
    refs = refs[25:]
    (w_qkv, w_o, w_gu, w_d, xs, qkv, probs, resid, factors, grads, picked_k, picked_v) = refs[:12]
    (raw, normed, attended, hidden, turned, hidden_t, y_low, wide, dh, f_low, d_att, gx) = refs[12:24]
    (sem_w, sem_in, sem_mem, sem_t, sem_out, sem_send, sem_recv) = refs[24:31]

    section, dpi, group = (lax.axis_index(name) for name in ("section", "dp", "group"))
    twin = (1 - section, dpi, group)
    is_lower = section == 0
    is_upper = section == 1
    scale = HEAD_DIM ** (-0.5)

    weights = []
    for i, (src, dst, pieces) in enumerate(
        ((w_qkv_hbm, w_qkv, 4), (w_o_hbm, w_o, 1), (w_gu_hbm, w_gu, 4), (w_d_hbm, w_d, 2))
    ):
        size = src.shape[0] // pieces
        weights.append(
            [
                pltpu.make_async_copy(src.at[pl.ds(p * size, size)], dst.at[pl.ds(p * size, size)], sem_w.at[i, p])
                for p in range(pieces)
            ]
        )

    def rows(m):
        return pl.ds(m * SEG, SEG)

    def load_tokens(m):
        return pltpu.make_async_copy(tokens.at[rows(m)], xs.at[m], sem_in.at[0, m])

    def load_cotangent(m):
        return pltpu.make_async_copy(cotangent.at[rows(m)], grads.at[m], sem_in.at[1, m])

    def send_up(m):
        return pltpu.make_async_remote_copy(
            src_ref=y_low.at[m], dst_ref=xs.at[m], send_sem=sem_send.at[0, m], recv_sem=sem_recv.at[0, m],
            device_id=twin, device_id_type=MESH,
        )

    def send_down(m):
        return pltpu.make_async_remote_copy(
            src_ref=gx.at[m], dst_ref=grads.at[m], send_sem=sem_send.at[1, m], recv_sem=sem_recv.at[1, m],
            device_id=twin, device_id_type=MESH,
        )

    @pl.when(is_lower)
    def _():
        load_tokens(0).start()

    for copy in weights[0]:
        copy.start()

    @pl.when(is_lower)
    def _():
        load_tokens(1).start()

    memory_in = [
        pltpu.make_async_copy(src, raw.at[i], sem_mem.at[i]) for i, src in enumerate((mem_k, mem_v))
    ]

    @pl.when(is_upper)
    def _():
        for copy in memory_in:
            copy.start()
        for m in range(MICRO):
            load_cotangent(m).start()

    for group_copies in weights[1:]:
        for copy in group_copies:
            copy.start()

    barrier = pltpu.get_barrier_semaphore()
    pl.semaphore_signal(barrier, inc=1, device_id=twin, device_id_type=MESH)
    pl.semaphore_wait(barrier, 1)

    @pl.when(is_lower)
    def _():
        picked_k[...] = jnp.zeros_like(picked_k)
        picked_v[...] = jnp.zeros_like(picked_v)

    @pl.when(is_upper)
    def _():
        for copy in memory_in:
            copy.wait()
        places = lax.broadcasted_iota(jnp.int32, (TOPM, SEG), 1)
        for m in range(MICRO):
            chosen = to_low(to_f32(index[m] == places))
            for n in range(4):
                picked_k[m, :, cols(n)] = to_low(times(chosen, raw[0, m, :, cols(n)]))
                picked_v[m, :, cols(n)] = to_low(times(chosen, raw[1, m, :, cols(n)]))

    eye = to_low(
        to_f32(
            lax.broadcasted_iota(jnp.int32, (BLOCK, BLOCK), 0) == lax.broadcasted_iota(jnp.int32, (BLOCK, BLOCK), 1)
        )
    )
    turned_copies = {}

    def turn(src, width, dst, slot, out, sem, m):
        if m:
            turned_copies[sem].wait()

        def step(j, _):
            dst[slot + (pl.ds(pl.multiple_of(j * BLOCK, BLOCK), BLOCK), slice(None))] = to_low(
                by_rows(eye, src[:, cols(j)])
            )
            return 0

        lax.fori_loop(0, width // BLOCK, step, 0, unroll=True)
        view = dst.at[slot[0]] if slot else dst
        turned_copies[sem] = pltpu.make_async_copy(view, out.at[:, cols(m)], sem_t.at[sem])
        turned_copies[sem].start()

    def forward(m):
        @pl.when(is_lower)
        def _():
            load_tokens(m).wait()

        @pl.when(is_upper)
        def _():
            send_up(m).wait_recv()

        x = to_f32(xs[m])
        normed[...] = to_low(x * inverse_rms(x) * gain_a[...])
        if m == 0:
            for copy in weights[0]:
                copy.wait()

        def rotated(j, _):
            block = times(normed[...], w_qkv[:, cols(j)])
            for p in range(2):
                part = block[:, p * HEAD_DIM : (p + 1) * HEAD_DIM]
                part = part * cosine[...] + pltpu.roll(part, HEAD_DIM // 2, 1) * sine[...]
                qkv[m, :, cols(2 * j + p, HEAD_DIM)] = to_low(part)
            return 0

        lax.fori_loop(0, 8, rotated, 0, unroll=4)

        def plain(j, _):
            qkv[m, :, cols(j, BLOCK, 2 * D)] = to_low(times(normed[...], w_qkv[:, cols(j, BLOCK, 2 * D)]))
            return 0

        lax.fori_loop(0, 4, plain, 0, unroll=True)
        turn(normed, D, turned, (0,), na_t, 0, m)
        causal = lax.broadcasted_iota(jnp.int32, (SEG, SEG), 0) >= lax.broadcasted_iota(jnp.int32, (SEG, SEG), 1)

        def head(h, _):
            query = qkv[m, :, cols(h, HEAD_DIM)]
            local = by_rows(query, qkv[m, :, cols(h, HEAD_DIM, D)]) * scale
            local = jnp.where(causal, local, NEG)
            remote = by_rows(query, picked_k[m, :, cols(h, HEAD_DIM)]) * scale + bias[m]
            peak = jnp.maximum(
                jnp.max(local, axis=-1, keepdims=True), jnp.max(remote, axis=-1, keepdims=True)
            )
            local = jnp.exp(local - peak)
            remote = jnp.exp(remote - peak)
            share = 1.0 / (jnp.sum(local, axis=-1, keepdims=True) + jnp.sum(remote, axis=-1, keepdims=True))
            local = to_low(local * share)
            remote = to_low(remote * share)
            probs[m, h, :, :SEG] = local
            probs[m, h, :, SEG:] = remote
            result = times(local, qkv[m, :, cols(h, HEAD_DIM, 2 * D)])
            result += times(remote, picked_v[m, :, cols(h, HEAD_DIM)])
            attended[:, cols(h, HEAD_DIM)] = to_low(result)
            return 0

        lax.fori_loop(0, HEADS, head, 0, unroll=4)
        if m == 0:
            weights[1][0].wait()

        def project(n, _):
            resid[m, :, cols(n)] = to_f32(xs[m, :, cols(n)]) + times(attended[...], w_o[:, cols(n)])
            return 0

        lax.fori_loop(0, 4, project, 0, unroll=True)
        turn(attended, D, turned, (1,), o_t, 1, m)
        h = resid[m]
        normed[...] = to_low(h * inverse_rms(h) * gain_f[...])
        if m == 0:
            for copy in weights[2]:
                copy.wait()

        def gate(j, _):
            a = times(normed[...], w_gu[:, cols(j)])
            u = times(normed[...], w_gu[:, cols(j, BLOCK, FF)])
            sg = jax.nn.sigmoid(a)
            silu = a * sg
            hidden[:, cols(j)] = to_low(silu * u)
            factors[m, :, cols(j)] = to_low(u * sg * (1.0 + a * (1.0 - sg)))
            factors[m, :, cols(j, BLOCK, FF)] = to_low(silu)
            return 0

        lax.fori_loop(0, FF // BLOCK, gate, 0, unroll=4)
        if m == 0:
            for copy in weights[3]:
                copy.wait()

        def down(n, _):
            y_low[m, :, cols(n)] = to_low(resid[m, :, cols(n)] + times(hidden[...], w_d[:, cols(n)]))
            return 0

        lax.fori_loop(0, 4, down, 0, unroll=2)

        @pl.when(is_lower)
        def _():
            send_up(m).start()

        write_out(y_low.at[m], act.at[rows(m)], 0, m).start()
        turn(normed, D, turned, (2,), nf_t, 2, m)
        turn(hidden, FF, hidden_t, (), z_t, 3, m)

    def write_out(src, dst, kind, m):
        return pltpu.make_async_copy(src, dst, sem_out.at[kind, m])

    def block_out(src, dst, kind, m, i):
        return write_out(src.at[m, :, cols(i)], dst.at[i, rows(m)], kind, m)

    block_sets = ((grads, e_cols, 2, 4), (factors, dgu, 3, 22), (f_low, f_cols, 4, 4), (qkv, dm, 5, 12))

    def start_blocks(which, m):
        src, dst, kind, count = block_sets[which]
        for i in range(count):
            block_out(src, dst, kind, m, i).start()

    def wait_blocks(which, m):
        src, dst, kind, count = block_sets[which]
        whole = dst.at[:, rows(m)]
        pltpu.make_async_copy(whole, whole, sem_out.at[kind, m]).wait()

    def norm_back(d_normed, values, gain, incoming):
        inverse = inverse_rms(values)
        scaled = d_normed * gain
        column = jnp.sum(d_normed * (values * inverse), axis=0, keepdims=True)
        centre = jnp.mean(scaled * values, axis=-1, keepdims=True)
        return incoming + inverse * scaled - values * (inverse * inverse * inverse * centre), column

    def backward(m):
        @pl.when(is_upper)
        def _():
            load_cotangent(m).wait()

        @pl.when(is_lower)
        def _():
            send_down(m).wait_recv()

        start_blocks(0, m)

        def gate_back(j, _):
            dz = by_rows(grads[m], w_d[pl.ds(pl.multiple_of(j * BLOCK, BLOCK), BLOCK), :])
            factors[m, :, cols(j)] = to_low(dz * to_f32(factors[m, :, cols(j)]))
            factors[m, :, cols(j, BLOCK, FF)] = to_low(dz * to_f32(factors[m, :, cols(j, BLOCK, FF)]))
            return 0

        lax.fori_loop(0, FF // BLOCK, gate_back, 0, unroll=4)
        start_blocks(1, m)

        def gate_up_back(n, _):
            wide[:, cols(n)] = by_rows(factors[m], w_gu[pl.ds(pl.multiple_of(n * BLOCK, BLOCK), BLOCK), :])
            return 0

        lax.fori_loop(0, 4, gate_up_back, 0)
        result, column = norm_back(wide[...], resid[m], gain_f[...], to_f32(grads[m]))
        dh[...] = result
        f_low[m] = to_low(result)
        gains[1:2, :] = column if m == 0 else gains[1:2, :] + column
        start_blocks(2, m)

        def out_back(n, _):
            d_att[:, cols(n)] = to_low(by_rows(f_low[m], w_o[pl.ds(pl.multiple_of(n * BLOCK, BLOCK), BLOCK), :]))
            return 0

        lax.fori_loop(0, 4, out_back, 0, unroll=True)

        def rotate_back(part):
            return part * cosine[...] - pltpu.roll(part, HEAD_DIM // 2, 1) * sine[...]

        def head_back(h, _):
            at_q, at_k, at_v = (cols(h, HEAD_DIM, base) for base in (0, D, 2 * D))
            query, key, value = qkv[m, :, at_q], qkv[m, :, at_k], qkv[m, :, at_v]
            d_out = d_att[:, cols(h, HEAD_DIM)]
            p_local = probs[m, h, :, :SEG]
            p_remote = probs[m, h, :, SEG:]
            d_local = by_rows(d_out, value)
            d_remote = by_rows(d_out, picked_v[m, :, cols(h, HEAD_DIM)])
            wide_local, wide_remote = to_f32(p_local), to_f32(p_remote)
            centre = jnp.sum(wide_local * d_local, axis=-1, keepdims=True) + jnp.sum(
                wide_remote * d_remote, axis=-1, keepdims=True
            )
            d_local = to_low(wide_local * (d_local - centre))
            d_remote = to_low(wide_remote * (d_remote - centre))
            d_query = (times(d_local, key) + times(d_remote, picked_k[m, :, cols(h, HEAD_DIM)])) * scale
            d_key = by_tokens(d_local, query) * scale
            qkv[m, :, at_v] = to_low(by_tokens(p_local, d_out))
            qkv[m, :, at_q] = to_low(rotate_back(d_query))
            qkv[m, :, at_k] = to_low(rotate_back(d_key))
            return 0

        lax.fori_loop(0, HEADS, head_back, 0, unroll=2)
        start_blocks(3, m)

        def qkv_back(n, _):
            wide[:, cols(n)] = by_rows(qkv[m], w_qkv[pl.ds(pl.multiple_of(n * BLOCK, BLOCK), BLOCK), :])
            return 0

        lax.fori_loop(0, 4, qkv_back, 0)
        result, column = norm_back(wide[...], to_f32(xs[m]), gain_a[...], dh[...])
        gx[m] = to_low(result)
        gains[0:1, :] = column if m == 0 else gains[0:1, :] + column

        @pl.when(is_upper)
        def _():
            send_down(m).start()

        write_out(gx.at[m], igrad.at[rows(m)], 1, m).start()

    gains[...] = jnp.zeros_like(gains)
    for m in range(MICRO):
        forward(m)
    for m in range(MICRO):
        backward(m)

    for m in range(MICRO):
        write_out(y_low.at[m], act.at[rows(m)], 0, m).wait()
        write_out(gx.at[m], igrad.at[rows(m)], 1, m).wait()
        for which in range(4):
            wait_blocks(which, m)
    for copy in turned_copies.values():
        copy.wait()

    @pl.when(is_lower)
    def _():
        for m in range(MICRO):
            send_up(m).wait_send()

    @pl.when(is_upper)
    def _():
        for m in range(MICRO):
            send_down(m).wait_send()


def rotary_constants():
    half = HEAD_DIM // 2
    freqs = np.exp(-np.log(10000.0) * np.arange(half) * 2.0 / HEAD_DIM)
    angles = np.arange(SEG)[:, None] * freqs[None, :]
    cosine = np.concatenate([np.cos(angles), np.cos(angles)], axis=1)
    sine = np.concatenate([-np.sin(angles), np.sin(angles)], axis=1)
    return cosine.astype(np.float32), sine.astype(np.float32)


def run_layers(tokens, cotangent, mem_keys, mem_values, index, bias, gain_a, gain_f, w_qkv, w_o, w_gu, w_d):
    cosine, sine = rotary_constants()
    count = tokens.shape[0]
    low, wide = jnp.bfloat16, jnp.float32
    anywhere = pl.BlockSpec(memory_space=pl.ANY)
    near_by = pl.BlockSpec(memory_space=pltpu.VMEM)
    shape = jax.ShapeDtypeStruct
    outs = (
        shape((count, D), low),
        shape((count, D), low),
        shape((D, count), low),
        shape((D, count), low),
        shape((D, count), low),
        shape((FF, count), low),
        shape((22, count, BLOCK), low),
        shape((12, count, BLOCK), low),
        shape((4, count, BLOCK), low),
        shape((4, count, BLOCK), low),
        shape((8, D), wide),
    )
    scratch = [
        pltpu.VMEM((D, 3 * D), low),
        pltpu.VMEM((D, D), low),
        pltpu.VMEM((D, 2 * FF), low),
        pltpu.VMEM((FF, D), low),
        pltpu.VMEM((MICRO, SEG, D), low),
        pltpu.VMEM((MICRO, SEG, 3 * D), low),
        pltpu.VMEM((MICRO, HEADS, SEG, SEG + TOPM), low),
        pltpu.VMEM((MICRO, SEG, D), wide),
        pltpu.VMEM((MICRO, SEG, 2 * FF), low),
        pltpu.VMEM((MICRO, SEG, D), low),
        pltpu.VMEM((MICRO, TOPM, D), low),
        pltpu.VMEM((MICRO, TOPM, D), low),
        pltpu.VMEM((2, MICRO, SEG, D), low),
        pltpu.VMEM((SEG, D), low),
        pltpu.VMEM((SEG, D), low),
        pltpu.VMEM((SEG, FF), low),
        pltpu.VMEM((3, D, SEG), low),
        pltpu.VMEM((FF, SEG), low),
        pltpu.VMEM((MICRO, SEG, D), low),
        pltpu.VMEM((SEG, D), wide),
        pltpu.VMEM((SEG, D), wide),
        pltpu.VMEM((MICRO, SEG, D), low),
        pltpu.VMEM((SEG, D), low),
        pltpu.VMEM((MICRO, SEG, D), low),
        pltpu.SemaphoreType.DMA((4, 4)),
        pltpu.SemaphoreType.DMA((2, MICRO)),
        pltpu.SemaphoreType.DMA((2,)),
        pltpu.SemaphoreType.DMA((4,)),
        pltpu.SemaphoreType.DMA((6, MICRO)),
        pltpu.SemaphoreType.DMA((2, MICRO)),
        pltpu.SemaphoreType.DMA((2, MICRO)),
    ]
    return pl.pallas_call(
        layer_kernel,
        out_shape=outs,
        in_specs=[anywhere] * 4 + [near_by] * 6 + [anywhere] * 4,
        out_specs=(anywhere,) * 10 + (near_by,),
        scratch_shapes=scratch,
        compiler_params=pltpu.CompilerParams(
            collective_id=1, has_side_effects=True, vmem_limit_bytes=60 * 2**20
        ),
        cost_estimate=pl.CostEstimate(flops=27 * 10**9, bytes_accessed=50 * 10**6, transcendentals=0),
        name="relay_layers",
    )(tokens, cotangent, mem_keys, mem_values, index, bias, cosine, sine, gain_a, gain_f, w_qkv, w_o, w_gu, w_d)


def finish_kernel(sq, down, gu_out, o_out, qkv_out, d_out, sq_v, d_v, gu_v, o_v, qkv_v, down_v, sem_in, sem_out):
    parts = (
        (gu_v, gu_out, 0, 11),
        (qkv_v, qkv_out, 13, 6),
        (o_v, o_out, 11, 2),
    )
    loads = [
        pltpu.make_async_copy(
            sq.at[:, pl.ds(base, count)], sq_v.at[:, pl.ds(base, count)], sem_in.at[i]
        )
        for i, (_, _, base, count) in enumerate(parts)
    ]
    load_d = pltpu.make_async_copy(down, d_v, sem_in.at[3])
    for copy in loads:
        copy.start()
    load_d.start()
    stores = []
    for i, (view, out, base, count) in enumerate(parts):
        loads[i].wait()
        for half in range(2):
            for c in range(count):
                at = pl.ds((half * count + c) * BLOCK, BLOCK)
                view[:, at] = sq_v[half, base + c].astype(jnp.float32)
            span = pl.ds(half * count * BLOCK, count * BLOCK)
            stores.append(pltpu.make_async_copy(view.at[:, span], out.at[:, span], sem_out.at[2 * i + half]))
            stores[-1].start()
    load_d.wait()
    for half in range(2):
        for k in range(4):
            down_v[pl.ds(half * 352, 352), pl.ds(k * BLOCK, BLOCK)] = d_v[half, k].astype(jnp.float32)
        span = pl.ds(half * 352, 352)
        stores.append(pltpu.make_async_copy(down_v.at[span], d_out.at[span], sem_out.at[6 + half]))
        stores[-1].start()
    for copy in stores:
        copy.wait()


def finish_gradients(out_sq, out_d):
    anywhere = pl.BlockSpec(memory_space=pl.ANY)
    shapes = ((256, 2 * FF), (256, D), (256, 3 * D), (704, D))
    return pl.pallas_call(
        finish_kernel,
        out_shape=tuple(jax.ShapeDtypeStruct(shape, jnp.float32) for shape in shapes),
        in_specs=[anywhere] * 2,
        out_specs=(anywhere,) * 4,
        scratch_shapes=[pltpu.VMEM(out_sq.shape, jnp.bfloat16), pltpu.VMEM(out_d.shape, jnp.bfloat16)]
        + [pltpu.VMEM(shape, jnp.float32) for shape in shapes]
        + [pltpu.SemaphoreType.DMA((4,)), pltpu.SemaphoreType.DMA((8,))],
        compiler_params=pltpu.CompilerParams(vmem_limit_bytes=40 * 2**20),
        name="finish_gradients",
    )(out_sq, out_d)


def body(
    group_size,
    tokens,
    cotangent,
    mem_keys,
    mem_values,
    mem_index,
    mem_flags,
    norm_attn,
    w_qkv,
    w_out,
    norm_ffn,
    w_gate_up,
    w_down,
):
    live = mem_flags * (lax.axis_index("section") == 1).astype(jnp.int32)
    bias = jnp.broadcast_to(jnp.where(live > 0, 0.0, NEG)[:, None, None], (MICRO, 1, TOPM))
    (act, igrad, na_t, nf_t, o_t, z_t, dgu, dm, f_cols, e_cols, gains) = run_layers(
        tokens,
        cotangent,
        mem_keys,
        mem_values,
        mem_index[:, :, None],
        bias.astype(jnp.float32),
        norm_attn.astype(jnp.float32),
        norm_ffn.astype(jnp.float32),
        w_qkv[0],
        w_out[0],
        w_gate_up[0],
        w_down[0],
    )
    out_sq, out_d, out_gains = reduce_gradients(
        group_size, nf_t, na_t, o_t, z_t.reshape(4, 2, 352, -1), dgu, dm, f_cols, e_cols, gains
    )
    grad_gu, grad_o, grad_qkv, grad_d = finish_gradients(out_sq, out_d)
    start = lax.axis_index("dp") * BLOCK
    gain_rows = lax.dynamic_slice(out_gains, (0, start), (2, BLOCK))
    return (
        act[None],
        igrad[None],
        gain_rows[0:1],
        grad_qkv[None],
        grad_o[None],
        gain_rows[1:2],
        grad_gu[None],
        grad_d[None],
    )


def solution(mesh):
    placed = (
        P(("dp", "group"), None),
        P(("dp", "group"), None),
        P(("dp", "group"), None, None),
        P(("dp", "group"), None, None),
        P(("dp", "group"), None),
        P(("dp", "group")),
        P("section", None),
        P("section", None, None),
        P("section", None, None),
        P("section", None),
        P("section", None, None),
        P("section", None, None),
    )
    return jax.shard_map(
        functools.partial(body, mesh.shape["group"]),
        mesh=mesh,
        in_specs=placed,
        out_specs=(
            P("section", ("dp", "group"), None),
            P("section", ("dp", "group"), None),
            P("section", "dp"),
            P("section", "dp", None),
            P("section", "dp", None),
            P("section", "dp"),
            P("section", "dp", None),
            P("section", "dp", None),
        ),
        check_vma=False,
    )
```

time: 724 us -> 400 us (0.55); the launches traced: 716 us -> 399 us
  local copies, waits for them, and re-layouts: 175 us -> 9.25 us
  Pallas kernels: 249 us -> 386 us
  other arithmetic: 104 us -> 3.22 us
  matrix products: 84.4 us -> 0 us
  waiting for transfers between devices: 80.1 us -> 0 us
  loops' own time: 12.8 us -> 0 us
    pallas_call x0 -> x2, Pallas kernels: none -> 110 us  [the longest x1 104 us: run_layers(): pl.pallas_call(layer_kernel, out_shape=outs, in_specs=[anywhere] * 4 + [n...]
    dot_general x40 -> x0, matrix products: 84.4 us -> none  [the longest x8 30 us: contract_cols(): lax.dot_general(left, right, (((1,), (1,)), ((), ())), preferred_element_...]
    ppermute x4 -> x0, waiting for transfers between devices: 80.1 us -> none  [from_behind(): return lax.ppermute(block, axis, route)]
    select_n x21 -> x1, other arithmetic: 41.8 us -> 0.66 us  [body(): jnp.where(live > 0, 0.0, NEG)[:, None, None]]
    another operation x40 -> x0, local copies, waits for them, and re-layouts: 36.7 us -> none
    convert_element_type x26 -> x2, other arithmetic: 34.3 us -> 2.57 us  [the longest x1 1.28 us: body(): norm_attn.astype(jnp.float32)]
    cond x125 -> x0, local copies, waits for them, and re-layouts: 31.4 us -> none  [the longest x8 14.9 us: body(): lax.cond(busy, forward_active, forward_spare, (layer_input, memory))]
    pallas_call x1, Pallas kernels: 249 us -> 276 us  [reduce_gradients(): pl.pallas_call(functools.partial(reduce_kernel, tuple(extra)), out_shape=...]
  transfers between devices with their start and end apart: 4 -> 0, of which waited for: 2 -> 0; matrix products, arithmetic and copies ran while one was open for 9% -> 0% of each run, Pallas kernels for 0% -> 0%
where the time goes in v2:
time: 400 us; the launch traced here: 399 us
  Pallas kernels  386 us (96%)
  local copies, waits for them, and re-layouts  9.25 us (2%)
    pallas_call x1, Pallas kernels, reduce_gradients(): pl.pallas_call(functools.partial(reduce_kernel, tuple(extra)), out_shape=...  276 us
    pallas_call x1, Pallas kernels, run_layers(): pl.pallas_call(layer_kernel, out_shape=outs, in_specs=[anywhere] * 4 + [n...  104 us

profile of v2, /device:TPU:0, one launch (start us, length us, event | category | flops | bytes accessed | tf_op | source)
XLA Modules:
  0.0 399.4 jit_solution(12564323322399463310)
XLA Ops:
  0.6 1.5 copy.22.refs_4_
  2.1 0.7 compare_select_fusion
  2.8 0.6 broadcast_in_dim.38.refs_5_
  3.4 1.3 convert_element_type.10.refs_8_
  4.7 1.3 convert_element_type.11.refs_9_
  6.0 104.3 %relay_layers.1 = (bf16[512,1024]{1,0:T(8,128)(2,1)}, bf16[512,1024]{1,0:T(8,128)(2,1)}, bf16[1024,512]{1,0:T(8,128)(2,1)}, bf16[1024,512]{1,0:T(8,128)(2,1)}, b...) custom-call(bf16[512,1024]{1,0:T(8,128)(2,1)} %refs_0_.1, ...), custom_call_target="tpu_custom_call" | custom-call | flops 27000000512 | bytes 50000000 | tf_op jit(solution)/shard_map/relay_layers/pallas_call | solution.py:803
  110.3 0.0 copy-start.3
  110.3 0.0 copy-start.2
  110.3 276.4 %reduce_gradients.1 = (bf16[2,19,256,256]{3,2,1,0:T(8,128)(2,1)}, bf16[2,4,352,256]{3,2,1,0:T(8,128)(2,1)}, f32[8,1024]{1,0:T(8,128)}) custom-call(bf16[1024,512]{1,0:T(8,128)(2,1)} %get-tuple-element.28.refs_0_, bf16[1024,512]{1,0:T(8,128)(2,1)} %get-tuple-element.29.refs_1_, bf16[1024,512]{1,0:T(8,128)(2,1)} %get-tuple-element.30.refs_2_, ...), custom_call_target="tpu_custom_call" | custom-call | flops 12999999488 | bytes 30000000 | tf_op jit(solution)/shard_map/reduce_gradients/pallas_call | solution.py:352
  386.7 1.4 fusion
  388.1 0.0 copy-start
  388.1 2.4 copy-done
  390.5 0.0 copy-start.1
  390.5 1.4 copy-done.1
  391.9 5.6 %finish_gradients.1 = (f32[256,5632]{1,0:T(8,128)}, f32[256,1024]{1,0:T(8,128)}, f32[256,3072]{1,0:T(8,128)}, f32[704,1024]{1,0:T(8,128)}) custom-call(bf16[2,19,256,256]{3,2,1,0:T(8,128)(2,1)S(1)} %copy-done, bf16[2,4,352,256]{3,2,1,0:T(8,128)(2,1)S(1)} %copy-done.1), custom_call_target="tpu_custom_call" | custom-call | tf_op jit(solution)/shard_map/finish_gradients/pallas_call | solution.py:857
  397.5 0.0 copy-done.3
  397.5 1.0 copy.25
  398.4 0.0 copy-done.2
  398.4 1.0 copy.26
Async XLA Ops:
  110.3 287.2 %copy-start.3 = (bf16[512,1024]{1,0:T(8,128)(2,1)S(1)}, bf16[512,1024]{1,0:T(8,128)(2,1)}, u32[]{:S(2)}) copy-start(bf16[512,1024]{1,0:T(8,128)(2,1)} %get-tuple-element.26) | copy-start | bytes 3145732
  110.3 288.2 %copy-start.2 = (bf16[512,1024]{1,0:T(8,128)(2,1)S(1)}, bf16[512,1024]{1,0:T(8,128)(2,1)}, u32[]{:S(2)}) copy-start(bf16[512,1024]{1,0:T(8,128)(2,1)} %get-tuple-element.27) | copy-start | bytes 3145732
  388.1 2.4 copy-start
  390.5 1.4 copy-start.1

commit v3 on v2

--- a/solution.py
+++ b/solution.py
@@ -32,15 +32,15 @@
 
 def reduce_kernel(extra, *refs):
     n_extra = len(extra)
-    (nf_t, na_t, o_t, z_t, dgu, dm, f_cols, e_cols, gains) = refs[:9]
-    (out_sq, out_d, out_gains) = refs[9:12]
-    refs = refs[12:]
+    (nf_t, na_t, o_t, z_t, dgu, dm, f_cols, e_cols, nf_p, na_p, o_p, z_p, dgu_p, e_p, gains) = refs[:15]
+    (out_sq, out_d, out_gains) = refs[15:18]
+    refs = refs[18:]
     (a_own, a_in, z_own, z_in, b_own, b_in, e_own, e_in) = refs[:8]
     (g_sq, q0, q1, q2, g_d, d0, d1, d2, gain_out, gain_in) = refs[8:18]
     refs = refs[18:]
     x_sq, x_d = refs[:2]
-    (sem_load, sem_bload, sem_asend, sem_arecv, sem_bsend, sem_brecv) = refs[2:8]
-    (sem_send, sem_recv, sem_copy, gain_send, gain_recv) = refs[8:13]
+    (sem_load, sem_bload, sem_bsend, sem_brecv) = refs[2:6]
+    (sem_send, sem_recv, sem_copy, gain_send, gain_recv) = refs[6:11]
 
     section, dpi, group = (lax.axis_index(name) for name in ("section", "dp", "group"))
     mask1 = 1 + section
@@ -67,55 +67,60 @@
         )
 
     def load_a(slot):
-        src = (nf_t, o_t, na_t)[slot]
-        return pltpu.make_async_copy(src, a_own.at[slot], sem_load.at[slot])
+        return (
+            pltpu.make_async_copy((nf_t, o_t, na_t)[slot], a_own.at[slot], sem_load.at[0, slot]),
+            pltpu.make_async_copy((nf_p, o_p, na_p)[slot], a_in.at[slot], sem_load.at[1, slot]),
+        )
 
     def load_z():
-        return pltpu.make_async_copy(z_t.at[pl.ds(0, 4), half], z_own, sem_load.at[3])
-
-    def b_src(index, part):
-        if index[0] == 0:
-            return dgu.at[part * 11 + index[1]]
-        if index[0] == 1:
-            return f_cols.at[part * 2 + index[1]]
-        return dm.at[part * 6 + index[1]]
-
-    def load_b(kind, i, slot):
-        return pltpu.make_async_copy(b_src((kind, i), half), b_own.at[slot], sem_bload.at[slot])
+        return (
+            pltpu.make_async_copy(z_t.at[pl.ds(0, 4), half], z_own, sem_load.at[0, 3]),
+            pltpu.make_async_copy(z_p, z_in, sem_load.at[1, 3]),
+        )
+
+    def load_gu(i):
+        return (
+            pltpu.make_async_copy(dgu.at[half * 11 + i], b_own.at[i], sem_bload.at[0, i]),
+            pltpu.make_async_copy(dgu_p.at[i], b_in.at[i], sem_bload.at[1, i]),
+        )
 
     def load_e(k):
-        return pltpu.make_async_copy(e_cols.at[k], e_own.at[k], sem_bload.at[19 + k])
-
-    def send_a(slot):
-        src = (nf_t, o_t, na_t)[slot]
-        return remote(src, a_in.at[slot], sem_asend.at[slot], sem_arecv.at[slot], first)
-
-    def send_z():
-        return remote(z_t.at[pl.ds(0, 4), 1 - half], z_in, sem_asend.at[3], sem_arecv.at[3], first)
-
-    def send_b(kind, i, slot):
-        return remote(b_src((kind, i), 1 - half), b_in.at[slot], sem_bsend.at[slot], sem_brecv.at[slot], first)
-
-    def send_e(k):
-        return remote(e_cols.at[k], e_in.at[k], sem_bsend.at[19 + k], sem_brecv.at[19 + k], first)
+        return (
+            pltpu.make_async_copy(e_cols.at[k], e_own.at[k], sem_bload.at[0, 19 + k]),
+            pltpu.make_async_copy(e_p.at[k], e_in.at[k], sem_bload.at[1, 19 + k]),
+        )
+
+    def late(part, i):
+        return f_cols.at[part * 2 + i] if i < 2 else dm.at[part * 6 + i - 2]
+
+    def load_late(i):
+        return pltpu.make_async_copy(late(half, i), b_own.at[11 + i], sem_bload.at[0, 11 + i])
+
+    def send_late(i):
+        return remote(late(1 - half, i), b_in.at[11 + i], sem_bsend.at[i], sem_brecv.at[i], first)
+
+    def start(copies):
+        for copy in copies:
+            copy.start()
+
+    def finish_copies(copies):
+        for copy in copies:
+            copy.wait()
 
     kinds = ((0, 0, 11), (1, 11, 2), (2, 13, 6))
-    load_z().start()
-    send_z().start()
-
-    @pl.loop(0, 4)
-    def _(k):
-        load_e(k).start()
-        send_e(k).start()
-
-    for kind, base, count in kinds:
-        load_a(kind).start()
-        send_a(kind).start()
-
-        @pl.loop(0, count)
-        def _(i):
-            load_b(kind, i, base + i).start()
-            send_b(kind, i, base + i).start()
+    start(load_z())
+    start(load_e(0))
+    for i in range(8):
+        send_late(i).start()
+    start(load_a(0))
+    for i in range(11):
+        start(load_gu(i))
+        if i in (2, 5, 8):
+            start(load_e(i // 3 + 1))
+    start(load_a(1))
+    start(load_a(2))
+    for i in range(8):
+        load_late(i).start()
 
     class Square:
         base, rows = 4, 256
@@ -125,21 +130,47 @@
         base, rows = 0, 352
         partial, recv0, recv1, recv2, xs, out = g_d, d0, d1, d2, x_d, out_d
 
-    def to_near(cls, c):
-        k = cls.base + c
-        return remote(cls.partial.at[c, pl.ds(0, 2), 1 - bit0], cls.recv0.at[c], sem_send.at[0, k], sem_recv.at[0, k], near)
-
-    def to_far(cls, c):
-        k = cls.base + c
-        return remote(cls.recv0.at[c, 1 - bit1], cls.recv1.at[c], sem_send.at[1, k], sem_recv.at[1, k], far)
-
     def rows_at(cls, part):
         size = cls.rows // 2
         return pl.ds(pl.multiple_of(part * size, 16), size)
 
-    def to_second(cls, c):
+    def hop(cls, c, i, src, dst, device):
         k = cls.base + c
-        return remote(cls.recv1.at[c, rows_at(cls, 1 - low2)], cls.recv2.at[c], sem_send.at[2, k], sem_recv.at[2, k], second)
+        return remote(src, dst, sem_send.at[i, k], sem_recv.at[i, k], device)
+
+    def hops(cls, c):
+        both = pl.ds(0, 2)
+        if cls is Down:
+            return (
+                lambda: hop(cls, c, 0, cls.partial.at[c, both, 1 - bit0], cls.recv0.at[c], near),
+                lambda: hop(cls, c, 1, cls.recv0.at[c, 1 - bit1], cls.recv1.at[c], far),
+                lambda: hop(cls, c, 2, cls.recv1.at[c, rows_at(cls, 1 - low2)], cls.recv2.at[c], second),
+            )
+        return (
+            lambda: hop(cls, c, 0, cls.partial.at[c, both, both, rows_at(cls, 1 - low2)], cls.recv0.at[c], second),
+            lambda: hop(cls, c, 1, cls.recv0.at[c, both, 1 - bit0], cls.recv1.at[c], near),
+            lambda: hop(cls, c, 2, cls.recv1.at[c, 1 - bit1], cls.recv2.at[c], far),
+        )
+
+    def combine(cls, c, i):
+        if cls is Down:
+            if i == 0:
+                for j in range(2):
+                    cls.recv0[c, j] = summed(cls.partial[c, j, bit0], cls.recv0[c, j])
+            elif i == 1:
+                cls.recv1[c] = summed(cls.recv0[c, bit1], cls.recv1[c])
+            else:
+                cls.recv2[c] = summed(cls.recv1[c, rows_at(cls, low2)], cls.recv2[c])
+        elif i == 0:
+            for j in range(4):
+                cls.recv0[c, j // 2, j % 2] = summed(
+                    cls.partial[c, j // 2, j % 2, rows_at(cls, low2)], cls.recv0[c, j // 2, j % 2]
+                )
+        elif i == 1:
+            for j in range(2):
+                cls.recv1[c, j] = summed(cls.recv0[c, j, bit0], cls.recv1[c, j])
+        else:
+            cls.recv2[c] = summed(cls.recv1[c, bit1], cls.recv2[c])
 
     def to_extra(cls, c, i):
         k = cls.base + c
@@ -175,11 +206,19 @@
 
             @pl.when(c == base)
             def _():
-                load_a(kind).wait()
-                send_a(kind).wait_recv()
-
-        load_b(0, 0, c).wait()
-        send_b(0, 0, c).wait_recv()
+                finish_copies(load_a(kind))
+
+        @pl.when(c < 11)
+        def _():
+            finish_copies(load_gu(c))
+
+        for i in range(8):
+
+            @pl.when(c == 11 + i)
+            def _():
+                load_late(i).wait()
+                send_late(i).wait_recv()
+
         for kind, base, count in kinds:
 
             @pl.when((c >= base) & (c < base + count))
@@ -190,40 +229,29 @@
                         a_own[kind, rows, :], b_own[c], a_in[kind, rows, :], b_in[c]
                     )
 
-        to_near(Square, c).start()
+        hops(Square, c)[0]().start()
 
     def partial_down(c):
         @pl.when(c == 0)
         def _():
-            load_z().wait()
-            send_z().wait_recv()
-
-        load_e(c).wait()
-        send_e(c).wait_recv()
+            finish_copies(load_z())
+
+        finish_copies(load_e(c))
         for j in range(4):
             g_d[c, j // 2, j % 2] = multiply(z_own[j], e_own[c], z_in[j], e_in[c])
-        to_near(Down, c).start()
-
-    def stage_near(cls, c):
-        to_near(cls, c).wait_recv()
-        for i in range(2):
-            cls.recv0[c, i] = summed(cls.partial[c, i, bit0], cls.recv0[c, i])
-        to_far(cls, c).start()
-
-    def stage_far(cls, c):
-        to_far(cls, c).wait_recv()
-        cls.recv1[c] = summed(cls.recv0[c, bit1], cls.recv1[c])
-        to_second(cls, c).start()
+        hops(Down, c)[0]().start()
 
     def share(cls, c):
         share_second(cls, c).start()
         share_first(cls, c).start()
         keep(cls, c).start()
 
-    def stage_second(cls, c):
-        to_second(cls, c).wait_recv()
-        cls.recv2[c] = summed(cls.recv1[c, rows_at(cls, low2)], cls.recv2[c])
-        if n_extra:
+    def stage_hop(i, cls, c):
+        hops(cls, c)[i]().wait_recv()
+        combine(cls, c, i)
+        if i < 2:
+            hops(cls, c)[i + 1]().start()
+        elif n_extra:
             to_extra(cls, c, 0).start()
         else:
             share(cls, c)
@@ -244,7 +272,7 @@
     def partial(cls, c):
         (partial_square if cls is Square else partial_down)(c)
 
-    stages = [partial, stage_near, stage_far, stage_second]
+    stages = [partial] + [functools.partial(stage_hop, i) for i in range(3)]
     stages += [functools.partial(lambda i, cls, c: stage_extra(cls, c, i), i) for i in range(n_extra)]
     stages += [stage_pass]
 
@@ -257,12 +285,19 @@
     def _(t):
         for i, stage in enumerate(stages):
             c = t - LAG * i
-
-            @pl.when((c >= 0) & (c < 4))
+            turn = c // 5
+
+            @pl.when((c >= 0) & (c < 20))
             def _():
-                stage(Down, c)
-
-            @pl.when((c >= 4) & (c < 23))
+                @pl.when(c % 5 == 0)
+                def _():
+                    stage(Down, turn)
+
+                @pl.when(c % 5 != 0)
+                def _():
+                    stage(Square, c - 1 - turn)
+
+            @pl.when((c >= 20) & (c < 23))
             def _():
                 stage(Square, c - 4)
 
@@ -281,14 +316,12 @@
     gain_exchange(last).wait()
     out_gains[...] = gain_out[last] + gain_in[last]
 
-    send_z().wait_send()
-    for kind, base, count in kinds:
-        send_a(kind).wait_send()
+    for i in range(8):
+        send_late(i).wait_send()
 
     def finish(cls, c):
-        to_near(cls, c).wait_send()
-        to_far(cls, c).wait_send()
-        to_second(cls, c).wait_send()
+        for make in hops(cls, c):
+            make().wait_send()
         share_second(cls, c).wait_send()
         share_first(cls, c).wait()
         pass_on(cls, c).wait()
@@ -296,16 +329,14 @@
 
     @pl.loop(0, 4)
     def _(c):
-        send_e(c).wait_send()
         finish(Down, c)
 
     @pl.loop(0, 19)
     def _(c):
-        send_b(0, 0, c).wait_send()
         finish(Square, c)
 
 
-def reduce_gradients(group_size, nf_t, na_t, o_t, z_t, dgu, dm, f_cols, e_cols, gains):
+def reduce_gradients(group_size, activations, gains):
     extra = []
     mask = 4
     while mask < group_size:
@@ -313,7 +344,7 @@
         mask *= 2
     n_extra = len(extra)
     low = jnp.bfloat16
-    tokens = nf_t.shape[1]
+    tokens = activations[0].shape[1]
     scratch = [
         pltpu.VMEM((3, D, tokens), low),
         pltpu.VMEM((3, D, tokens), low),
@@ -324,8 +355,8 @@
         pltpu.VMEM((4, tokens, BLOCK), low),
         pltpu.VMEM((4, tokens, BLOCK), low),
         pltpu.VMEM((19, 2, 2, 256, BLOCK), low),
-        pltpu.VMEM((19, 2, 256, BLOCK), low),
-        pltpu.VMEM((19, 256, BLOCK), low),
+        pltpu.VMEM((19, 2, 2, 128, BLOCK), low),
+        pltpu.VMEM((19, 2, 128, BLOCK), low),
         pltpu.VMEM((19, 128, BLOCK), low),
         pltpu.VMEM((4, 2, 2, 352, BLOCK), low),
         pltpu.VMEM((4, 2, 352, BLOCK), low),
@@ -335,12 +366,10 @@
         pltpu.VMEM((4 + n_extra, 8, D), jnp.float32),
         pltpu.VMEM((max(n_extra, 1), 19 if n_extra else 1, 128, BLOCK), low),
         pltpu.VMEM((max(n_extra, 1), 4 if n_extra else 1, 176, BLOCK), low),
-        pltpu.SemaphoreType.DMA((4,)),
-        pltpu.SemaphoreType.DMA((23,)),
-        pltpu.SemaphoreType.DMA((4,)),
-        pltpu.SemaphoreType.DMA((4,)),
-        pltpu.SemaphoreType.DMA((23,)),
-        pltpu.SemaphoreType.DMA((23,)),
+        pltpu.SemaphoreType.DMA((2, 4)),
+        pltpu.SemaphoreType.DMA((2, 23)),
+        pltpu.SemaphoreType.DMA((8,)),
+        pltpu.SemaphoreType.DMA((8,)),
         pltpu.SemaphoreType.DMA((6 + n_extra, 23)),
         pltpu.SemaphoreType.DMA((6 + n_extra, 23)),
         pltpu.SemaphoreType.DMA((23,)),
@@ -356,7 +385,7 @@
             jax.ShapeDtypeStruct((2, 4, 352, BLOCK), low),
             jax.ShapeDtypeStruct((8, D), jnp.float32),
         ),
-        in_specs=[anywhere] * 8 + [near_by],
+        in_specs=[anywhere] * 14 + [near_by],
         out_specs=(anywhere, anywhere, near_by),
         scratch_shapes=scratch,
         compiler_params=pltpu.CompilerParams(
@@ -364,7 +393,7 @@
         ),
         cost_estimate=pl.CostEstimate(flops=13 * 10**9, bytes_accessed=30 * 10**6, transcendentals=0),
         name="reduce_gradients",
-    )(nf_t, na_t, o_t, z_t, dgu, dm, f_cols, e_cols, gains)
+    )(*activations, gains)
 
 
 def to_f32(value):
@@ -396,16 +425,20 @@
 
 
 def layer_kernel(*refs):
-    (tokens, cotangent, mem_k, mem_v, index, bias, cosine, sine, gain_a, gain_f) = refs[:10]
+    (tokens, cotangent, mem_k, mem_v, index, flags, cosine, sine, gain_a, gain_f) = refs[:10]
     (w_qkv_hbm, w_o_hbm, w_gu_hbm, w_d_hbm) = refs[10:14]
-    (act, igrad, na_t, nf_t, o_t, z_t, dgu, dm, f_cols, e_cols, gains) = refs[14:25]
-    refs = refs[25:]
+    (act, igrad, na_t, nf_t, o_t, z_t, dgu, dm, f_cols, e_cols) = refs[14:24]
+    (na_p, nf_p, o_p, z_p, dgu_p, e_p, gains) = refs[24:31]
+    refs = refs[31:]
     (w_qkv, w_o, w_gu, w_d, xs, qkv, probs, resid, factors, grads, picked_k, picked_v) = refs[:12]
-    (raw, normed, attended, hidden, turned, hidden_t, y_low, wide, dh, f_low, d_att, gx) = refs[12:24]
-    (sem_w, sem_in, sem_mem, sem_t, sem_out, sem_send, sem_recv) = refs[24:31]
+    (normed, attended, hidden, turned, hidden_t, y_low, wide, dh, f_low, d_att, gx) = refs[12:23]
+    (sem_w, sem_in, sem_mem, sem_t, sem_out, sem_send, sem_recv, sem_xsend, sem_xrecv) = refs[23:32]
 
     section, dpi, group = (lax.axis_index(name) for name in ("section", "dp", "group"))
+    mask1 = 1 + section
+    half = (group // mask1) % 2
     twin = (1 - section, dpi, group)
+    first = (section, dpi, flip(group, mask1))
     is_lower = section == 0
     is_upper = section == 1
     scale = HEAD_DIM ** (-0.5)
@@ -455,7 +488,9 @@
         load_tokens(1).start()
 
     memory_in = [
-        pltpu.make_async_copy(src, raw.at[i], sem_mem.at[i]) for i, src in enumerate((mem_k, mem_v))
+        pltpu.make_async_copy(src.at[m], factors.at[m, :, cols(i, D)], sem_mem.at[i, m])
+        for m in range(MICRO)
+        for i, src in enumerate((mem_k, mem_v))
     ]
 
     @pl.when(is_upper)
@@ -471,7 +506,8 @@
 
     barrier = pltpu.get_barrier_semaphore()
     pl.semaphore_signal(barrier, inc=1, device_id=twin, device_id_type=MESH)
-    pl.semaphore_wait(barrier, 1)
+    pl.semaphore_signal(barrier, inc=1, device_id=first, device_id_type=MESH)
+    pl.semaphore_wait(barrier, 2)
 
     @pl.when(is_lower)
     def _():
@@ -482,34 +518,45 @@
     def _():
         for copy in memory_in:
             copy.wait()
-        places = lax.broadcasted_iota(jnp.int32, (TOPM, SEG), 1)
+        places = lax.broadcasted_iota(jnp.int32, (SEG, TOPM), 0)
         for m in range(MICRO):
-            chosen = to_low(to_f32(index[m] == places))
+            chosen = to_low(to_f32(index[m : m + 1, :] == places).T)
             for n in range(4):
-                picked_k[m, :, cols(n)] = to_low(times(chosen, raw[0, m, :, cols(n)]))
-                picked_v[m, :, cols(n)] = to_low(times(chosen, raw[1, m, :, cols(n)]))
+                picked_k[m, :, cols(n)] = to_low(times(chosen, factors[m, :, cols(n)]))
+                picked_v[m, :, cols(n)] = to_low(times(chosen, factors[m, :, cols(n, BLOCK, D)]))
 
     eye = to_low(
         to_f32(
             lax.broadcasted_iota(jnp.int32, (BLOCK, BLOCK), 0) == lax.broadcasted_iota(jnp.int32, (BLOCK, BLOCK), 1)
         )
     )
-    turned_copies = {}
-
-    def turn(src, width, dst, slot, out, sem, m):
-        if m:
-            turned_copies[sem].wait()
-
+    sent = []
+
+    def exchange(src, dst, at):
+        copy = pltpu.make_async_remote_copy(
+            src_ref=src, dst_ref=dst, send_sem=sem_xsend.at[at], recv_sem=sem_xrecv.at[at],
+            device_id=first, device_id_type=MESH,
+        )
+        copy.start()
+        sent.append(copy)
+
+    def local(src, dst, sem):
+        copy = pltpu.make_async_copy(src, dst, sem)
+        copy.start()
+        sent.append(copy)
+
+    def turn(src, width, view, out, kind, m):
         def step(j, _):
-            dst[slot + (pl.ds(pl.multiple_of(j * BLOCK, BLOCK), BLOCK), slice(None))] = to_low(
-                by_rows(eye, src[:, cols(j)])
-            )
+            view[pl.ds(pl.multiple_of(j * BLOCK, BLOCK), BLOCK), :] = to_low(by_rows(eye, src[:, cols(j)]))
             return 0
 
         lax.fori_loop(0, width // BLOCK, step, 0, unroll=True)
-        view = dst.at[slot[0]] if slot else dst
-        turned_copies[sem] = pltpu.make_async_copy(view, out.at[:, cols(m)], sem_t.at[sem])
-        turned_copies[sem].start()
+        local(view, out.at[:, cols(m)], sem_t.at[kind, m])
+
+    def turn_square(src, kind, out, partner_out, m):
+        view = turned.at[m, kind]
+        turn(src, D, view, out, kind, m)
+        exchange(view, partner_out.at[:, cols(m)], kind * MICRO + m)
 
     def forward(m):
         @pl.when(is_lower)
@@ -521,7 +568,7 @@
             send_up(m).wait_recv()
 
         x = to_f32(xs[m])
-        normed[...] = to_low(x * inverse_rms(x) * gain_a[...])
+        normed[...] = to_low(x * inverse_rms(x) * to_f32(gain_a[...]))
         if m == 0:
             for copy in weights[0]:
                 copy.wait()
@@ -541,14 +588,15 @@
             return 0
 
         lax.fori_loop(0, 4, plain, 0, unroll=True)
-        turn(normed, D, turned, (0,), na_t, 0, m)
+        turn_square(normed, 0, na_t, na_p, m)
+        bias = (1 - flags[m] * section).astype(jnp.float32) * NEG
         causal = lax.broadcasted_iota(jnp.int32, (SEG, SEG), 0) >= lax.broadcasted_iota(jnp.int32, (SEG, SEG), 1)
 
         def head(h, _):
             query = qkv[m, :, cols(h, HEAD_DIM)]
             local = by_rows(query, qkv[m, :, cols(h, HEAD_DIM, D)]) * scale
             local = jnp.where(causal, local, NEG)
-            remote = by_rows(query, picked_k[m, :, cols(h, HEAD_DIM)]) * scale + bias[m]
+            remote = by_rows(query, picked_k[m, :, cols(h, HEAD_DIM)]) * scale + bias
             peak = jnp.maximum(
                 jnp.max(local, axis=-1, keepdims=True), jnp.max(remote, axis=-1, keepdims=True)
             )
@@ -573,9 +621,9 @@
             return 0
 
         lax.fori_loop(0, 4, project, 0, unroll=True)
-        turn(attended, D, turned, (1,), o_t, 1, m)
+        turn_square(attended, 1, o_t, o_p, m)
         h = resid[m]
-        normed[...] = to_low(h * inverse_rms(h) * gain_f[...])
+        normed[...] = to_low(h * inverse_rms(h) * to_f32(gain_f[...]))
         if m == 0:
             for copy in weights[2]:
                 copy.wait()
@@ -606,8 +654,13 @@
             send_up(m).start()
 
         write_out(y_low.at[m], act.at[rows(m)], 0, m).start()
-        turn(normed, D, turned, (2,), nf_t, 2, m)
-        turn(hidden, FF, hidden_t, (), z_t, 3, m)
+        turn_square(normed, 2, nf_t, nf_p, m)
+        turn(hidden, FF, hidden_t.at[m], z_t, 3, m)
+        for j in range(4):
+            at = pl.multiple_of(704 * j + 352 * (1 - half), 16)
+            exchange(
+                hidden_t.at[m, pl.ds(at, 352)], z_p.at[j, :, cols(m)], 3 * MICRO + 4 * m + j
+            )
 
     def write_out(src, dst, kind, m):
         return pltpu.make_async_copy(src, dst, sem_out.at[kind, m])
@@ -629,7 +682,7 @@
 
     def norm_back(d_normed, values, gain, incoming):
         inverse = inverse_rms(values)
-        scaled = d_normed * gain
+        scaled = d_normed * to_f32(gain)
         column = jnp.sum(d_normed * (values * inverse), axis=0, keepdims=True)
         centre = jnp.mean(scaled * values, axis=-1, keepdims=True)
         return incoming + inverse * scaled - values * (inverse * inverse * inverse * centre), column
@@ -644,6 +697,8 @@
             send_down(m).wait_recv()
 
         start_blocks(0, m)
+        for i in range(4):
+            exchange(grads.at[m, :, cols(i)], e_p.at[i, rows(m)], 14 + m * 15 + i)
 
         def gate_back(j, _):
             dz = by_rows(grads[m], w_d[pl.ds(pl.multiple_of(j * BLOCK, BLOCK), BLOCK), :])
@@ -653,6 +708,11 @@
 
         lax.fori_loop(0, FF // BLOCK, gate_back, 0, unroll=4)
         start_blocks(1, m)
+        for i in range(11):
+            exchange(
+                factors.at[m, :, cols((1 - half) * 11 + i)], dgu_p.at[i, rows(m)], 18 + m * 15 + i
+            )
+
 
         def gate_up_back(n, _):
             wide[:, cols(n)] = by_rows(factors[m], w_gu[pl.ds(pl.multiple_of(n * BLOCK, BLOCK), BLOCK), :])
@@ -724,7 +784,7 @@
         write_out(gx.at[m], igrad.at[rows(m)], 1, m).wait()
         for which in range(4):
             wait_blocks(which, m)
-    for copy in turned_copies.values():
+    for copy in sent:
         copy.wait()
 
     @pl.when(is_lower)
@@ -747,7 +807,7 @@
     return cosine.astype(np.float32), sine.astype(np.float32)
 
 
-def run_layers(tokens, cotangent, mem_keys, mem_values, index, bias, gain_a, gain_f, w_qkv, w_o, w_gu, w_d):
+def run_layers(tokens, cotangent, mem_keys, mem_values, index, flags, gain_a, gain_f, w_qkv, w_o, w_gu, w_d):
     cosine, sine = rotary_constants()
     count = tokens.shape[0]
     low, wide = jnp.bfloat16, jnp.float32
@@ -765,6 +825,12 @@
         shape((12, count, BLOCK), low),
         shape((4, count, BLOCK), low),
         shape((4, count, BLOCK), low),
+        shape((D, count), low),
+        shape((D, count), low),
+        shape((D, count), low),
+        shape((4, 352, count), low),
+        shape((11, count, BLOCK), low),
+        shape((4, count, BLOCK), low),
         shape((8, D), wide),
     )
     scratch = [
@@ -780,12 +846,11 @@
         pltpu.VMEM((MICRO, SEG, D), low),
         pltpu.VMEM((MICRO, TOPM, D), low),
         pltpu.VMEM((MICRO, TOPM, D), low),
-        pltpu.VMEM((2, MICRO, SEG, D), low),
         pltpu.VMEM((SEG, D), low),
         pltpu.VMEM((SEG, D), low),
         pltpu.VMEM((SEG, FF), low),
-        pltpu.VMEM((3, D, SEG), low),
-        pltpu.VMEM((FF, SEG), low),
+        pltpu.VMEM((MICRO, 3, D, SEG), low),
+        pltpu.VMEM((MICRO, FF, SEG), low),
         pltpu.VMEM((MICRO, SEG, D), low),
         pltpu.VMEM((SEG, D), wide),
         pltpu.VMEM((SEG, D), wide),
@@ -794,27 +859,35 @@
         pltpu.VMEM((MICRO, SEG, D), low),
         pltpu.SemaphoreType.DMA((4, 4)),
         pltpu.SemaphoreType.DMA((2, MICRO)),
-        pltpu.SemaphoreType.DMA((2,)),
-        pltpu.SemaphoreType.DMA((4,)),
+        pltpu.SemaphoreType.DMA((2, MICRO)),
+        pltpu.SemaphoreType.DMA((4, MICRO)),
         pltpu.SemaphoreType.DMA((6, MICRO)),
         pltpu.SemaphoreType.DMA((2, MICRO)),
         pltpu.SemaphoreType.DMA((2, MICRO)),
+        pltpu.SemaphoreType.DMA((44,)),
+        pltpu.SemaphoreType.DMA((44,)),
     ]
     return pl.pallas_call(
         layer_kernel,
         out_shape=outs,
-        in_specs=[anywhere] * 4 + [near_by] * 6 + [anywhere] * 4,
-        out_specs=(anywhere,) * 10 + (near_by,),
+        in_specs=[anywhere] * 4
+        + [near_by, pl.BlockSpec(memory_space=pltpu.SMEM)]
+        + [near_by] * 4
+        + [anywhere] * 4,
+        out_specs=(anywhere,) * 16 + (near_by,),
         scratch_shapes=scratch,
         compiler_params=pltpu.CompilerParams(
             collective_id=1, has_side_effects=True, vmem_limit_bytes=60 * 2**20
         ),
         cost_estimate=pl.CostEstimate(flops=27 * 10**9, bytes_accessed=50 * 10**6, transcendentals=0),
         name="relay_layers",
-    )(tokens, cotangent, mem_keys, mem_values, index, bias, cosine, sine, gain_a, gain_f, w_qkv, w_o, w_gu, w_d)
-
-
-def finish_kernel(sq, down, gu_out, o_out, qkv_out, d_out, sq_v, d_v, gu_v, o_v, qkv_v, down_v, sem_in, sem_out):
+    )(tokens, cotangent, mem_keys, mem_values, index, flags, cosine, sine, gain_a, gain_f, w_qkv, w_o, w_gu, w_d)
+
+
+def finish_kernel(*refs):
+    (sq, down, gains, act, igrad) = refs[:5]
+    (gu_out, o_out, qkv_out, d_out, ga_out, gf_out, act_out, igrad_out) = refs[5:13]
+    (sq_v, d_v, gu_v, o_v, qkv_v, down_v, sem_in, sem_out) = refs[13:]
     parts = (
         (gu_v, gu_out, 0, 11),
         (qkv_v, qkv_out, 13, 6),
@@ -830,7 +903,15 @@
     for copy in loads:
         copy.start()
     load_d.start()
-    stores = []
+    stores = [
+        pltpu.make_async_copy(act, act_out, sem_out.at[8]),
+        pltpu.make_async_copy(igrad, igrad_out, sem_out.at[9]),
+    ]
+    for copy in stores:
+        copy.start()
+    mine = cols(lax.axis_index("dp"))
+    ga_out[...] = gains[0:1, mine]
+    gf_out[...] = gains[1:2, mine]
     for i, (view, out, base, count) in enumerate(parts):
         loads[i].wait()
         for half in range(2):
@@ -851,20 +932,23 @@
         copy.wait()
 
 
-def finish_gradients(out_sq, out_d):
+def finish_gradients(out_sq, out_d, out_gains, act, igrad):
     anywhere = pl.BlockSpec(memory_space=pl.ANY)
+    near_by = pl.BlockSpec(memory_space=pltpu.VMEM)
     shapes = ((256, 2 * FF), (256, D), (256, 3 * D), (704, D))
+    wide = jnp.float32
     return pl.pallas_call(
         finish_kernel,
-        out_shape=tuple(jax.ShapeDtypeStruct(shape, jnp.float32) for shape in shapes),
-        in_specs=[anywhere] * 2,
-        out_specs=(anywhere,) * 4,
+        out_shape=tuple(jax.ShapeDtypeStruct(shape, wide) for shape in shapes + ((1, BLOCK),) * 2)
+        + (jax.ShapeDtypeStruct(act.shape, act.dtype),) * 2,
+        in_specs=[anywhere] * 2 + [near_by] + [anywhere] * 2,
+        out_specs=(anywhere,) * 4 + (near_by,) * 2 + (anywhere,) * 2,
         scratch_shapes=[pltpu.VMEM(out_sq.shape, jnp.bfloat16), pltpu.VMEM(out_d.shape, jnp.bfloat16)]
-        + [pltpu.VMEM(shape, jnp.float32) for shape in shapes]
-        + [pltpu.SemaphoreType.DMA((4,)), pltpu.SemaphoreType.DMA((8,))],
+        + [pltpu.VMEM(shape, wide) for shape in shapes]
+        + [pltpu.SemaphoreType.DMA((4,)), pltpu.SemaphoreType.DMA((10,))],
         compiler_params=pltpu.CompilerParams(vmem_limit_bytes=40 * 2**20),
         name="finish_gradients",
-    )(out_sq, out_d)
+    )(out_sq, out_d, out_gains, act, igrad)
 
 
 def body(
@@ -882,35 +966,34 @@
     w_gate_up,
     w_down,
 ):
-    live = mem_flags * (lax.axis_index("section") == 1).astype(jnp.int32)
-    bias = jnp.broadcast_to(jnp.where(live > 0, 0.0, NEG)[:, None, None], (MICRO, 1, TOPM))
-    (act, igrad, na_t, nf_t, o_t, z_t, dgu, dm, f_cols, e_cols, gains) = run_layers(
+    (act, igrad, na_t, nf_t, o_t, z_t, dgu, dm, f_cols, e_cols, na_p, nf_p, o_p, z_p, dgu_p, e_p, gains) = run_layers(
         tokens,
         cotangent,
         mem_keys,
         mem_values,
-        mem_index[:, :, None],
-        bias.astype(jnp.float32),
-        norm_attn.astype(jnp.float32),
-        norm_ffn.astype(jnp.float32),
+        mem_index,
+        mem_flags,
+        norm_attn,
+        norm_ffn,
         w_qkv[0],
         w_out[0],
         w_gate_up[0],
         w_down[0],
     )
-    out_sq, out_d, out_gains = reduce_gradients(
-        group_size, nf_t, na_t, o_t, z_t.reshape(4, 2, 352, -1), dgu, dm, f_cols, e_cols, gains
+    halves = z_t.reshape(4, 2, 352, -1)
+    reduced = reduce_gradients(
+        group_size,
+        (nf_t, na_t, o_t, halves, dgu, dm, f_cols, e_cols, nf_p, na_p, o_p, z_p, dgu_p, e_p),
+        gains,
     )
-    grad_gu, grad_o, grad_qkv, grad_d = finish_gradients(out_sq, out_d)
-    start = lax.axis_index("dp") * BLOCK
-    gain_rows = lax.dynamic_slice(out_gains, (0, start), (2, BLOCK))
+    (grad_gu, grad_o, grad_qkv, grad_d, grad_na, grad_nf, act, igrad) = finish_gradients(*reduced, act, igrad)
     return (
         act[None],
         igrad[None],
-        gain_rows[0:1],
+        grad_na,
         grad_qkv[None],
         grad_o[None],
-        gain_rows[1:2],
+        grad_nf,
         grad_gu[None],
         grad_d[None],
     )

time: 400 us -> 291 us (0.73)
  Pallas kernels: 386 us -> 285 us
  local copies, waits for them, and re-layouts: 9.25 us -> 4.53 us
    pallas_call x1, Pallas kernels: 276 us -> 160 us  [reduce_gradients(): pl.pallas_call(functools.partial(reduce_kernel, tuple(extra)), out_shape=...]
    pallas_call x1, Pallas kernels: 104 us -> 119 us  [run_layers(): pl.pallas_call(layer_kernel, out_shape=outs, in_specs=[anywhere] * 4 + [n...]
where the time goes in v3:
time: 291 us; the launch traced here: 290 us
  Pallas kernels  285 us (98%)
  local copies, waits for them, and re-layouts  4.53 us (2%)
    pallas_call x1, Pallas kernels, reduce_gradients(): pl.pallas_call(functools.partial(reduce_kernel, tuple(extra)), out_shape=...  160 us
    pallas_call x1, Pallas kernels, run_layers(): pl.pallas_call(layer_kernel, out_shape=outs, in_specs=[anywhere] * 4 + [n...  119 us
    pallas_call x1, Pallas kernels, finish_gradients(): pl.pallas_call(finish_kernel, out_shape=tuple((jax.ShapeDtypeStruct(shape...  6.57 us

profile of v3, /device:TPU:0, one launch (start us, length us, event | category | flops | bytes accessed | tf_op | source)
XLA Modules:
  0.0 290.5 jit_solution(12412310434876311845)
XLA Ops:
  0.6 119.0 %relay_layers.1 = (bf16[512,1024]{1,0:T(8,128)(2,1)}, bf16[512,1024]{1,0:T(8,128)(2,1)}, bf16[1024,512]{1,0:T(8,128)(2,1)}, bf16[1024,512]{1,0:T(8,128)(2,1)}, b...) custom-call(bf16[512,1024]{1,0:T(8,128)(2,1)} %refs_0_.1, ...), custom_call_target="tpu_custom_call" | custom-call | flops 27000000512 | bytes 50000000 | tf_op jit(solution)/shard_map/relay_layers/pallas_call | solution.py:870
  119.6 0.0 copy-start.2
  119.6 0.0 copy-start.3
  119.6 159.5 %reduce_gradients.1 = (bf16[2,19,256,256]{3,2,1,0:T(8,128)(2,1)}, bf16[2,4,352,256]{3,2,1,0:T(8,128)(2,1)}, f32[8,1024]{1,0:T(8,128)}) custom-call(bf16[1024,512]{1,0:T(8,128)(2,1)} %get-tuple-element.36.refs_0_, bf16[1024,512]{1,0:T(8,128)(2,1)} %get-tuple-element.37.refs_1_, bf16[1024,512]{1,0:T(8,128)(2,1)} %get-tuple-element.38.refs_2_, ...), custom_call_target="tpu_custom_call" | custom-call | flops 12999999488 | bytes 30000000 | tf_op jit(solution)/shard_map/reduce_gradients/pallas_call | solution.py:381
  279.2 0.0 copy-done.2
  279.2 0.0 copy-done.3
  279.2 0.0 copy-start
  279.2 2.4 copy-done
  281.6 0.0 copy-start.1
  281.6 1.4 copy-done.1
  283.0 0.0 copy-start.4
  283.0 0.8 copy-done.4
  283.7 6.6 %finish_gradients.1 = (f32[256,5632]{1,0:T(8,128)}, f32[256,1024]{1,0:T(8,128)}, f32[256,3072]{1,0:T(8,128)}, f32[704,1024]{1,0:T(8,128)}, f32[1,256]{1,0:T(1,12...) custom-call(bf16[2,19,256,256]{3,2,1,0:T(8,128)(2,1)S(1)} %copy-done, ...), custom_call_target="tpu_custom_call" | custom-call | tf_op jit(solution)/shard_map/finish_gradients/pallas_call | solution.py:940
Async XLA Ops:
  119.6 159.6 %copy-start.2 = (bf16[512,1024]{1,0:T(8,128)(2,1)S(1)}, bf16[512,1024]{1,0:T(8,128)(2,1)}, u32[]{:S(2)}) copy-start(bf16[512,1024]{1,0:T(8,128)(2,1)} %get-tuple-element.54.refs_3_) | copy-start | bytes 3145732
  119.6 159.6 %copy-start.3 = (bf16[512,1024]{1,0:T(8,128)(2,1)S(1)}, bf16[512,1024]{1,0:T(8,128)(2,1)}, u32[]{:S(2)}) copy-start(bf16[512,1024]{1,0:T(8,128)(2,1)} %get-tuple-element.55.refs_4_) | copy-start | bytes 3145732
  279.2 2.4 copy-start
  281.6 1.4 copy-start.1
  283.0 0.8 copy-start.4
